TPU v7x, 32 devices: a whole 2x2x4 slice. The times are simulated.
32 devices in a mesh: dp: 8 (over y, x, core), seq: 4 (over z).
Axes of the slice: x: 2, y: 2, z: 4, core: 2. Of those that a mesh axis runs over, the one named last changes fastest.
Arguments:
- tokens: bfloat16 [32768, 1024], P(('dp', 'seq')), may hold values from -6 to 6
- norm_gain: float32 [1024], replicated, may hold values from 0.4 to 1.6
- in_proj: bfloat16 [1024, 4384], P('dp'), may hold values from -0.1875 to 0.1875
- conv_weight: float32 [4, 2304], replicated, may hold values from -3 to 3
- conv_bias: float32 [2304], replicated, may hold values from -3 to 3
- dt_bias: float32 [32], replicated, may hold values from -6 to -2
- a_log: float32 [32], replicated, may hold values from -1.5 to 2.5
- skip_d: float32 [32], replicated, may hold values from 0.5 to 1.5
- gate_norm: float32 [2048], replicated, may hold values from 0.4 to 1.6
- out_proj: bfloat16 [2048, 1024], P('dp'), may hold values from -0.125 to 0.125
- cotangent: bfloat16 [32768, 1024], P(('dp', 'seq')), may hold values from -6 to 6
Outputs:
- block_out: bfloat16 [32768, 1024], P(('dp', 'seq'))
- input_grad: bfloat16 [32768, 1024], P(('dp', 'seq'))
- norm_gain_grad: float32 [1024], replicated
- in_proj_grad: float32 [1024, 4384], P('dp', 'seq')
- conv_weight_grad: float32 [4, 2304], replicated
- conv_bias_grad: float32 [2304], replicated
- dt_bias_grad: float32 [32], replicated
- a_log_grad: float32 [32], replicated
- skip_grad: float32 [32], replicated
- gate_norm_grad: float32 [2048], replicated
- out_proj_grad: float32 [2048, 1024], P('dp', 'seq')
All inputs are finite; a program needn't handle non-finite values.
Results may differ from a plain program's by a relative error of at most 0.011.
Values may be sent and summed in bfloat16 or wider, within the bound.
A program may use at most 256 MiB of HBM per device.

v0:
```python
from functools import partial

import jax
import jax.numpy as jnp
from jax import lax
from jax.sharding import PartitionSpec as P

BLOCK = 256


epsilon = 1e-05
highest = lax.Precision.HIGHEST


def passed_along(block, axis, distance):
    devices = range(lax.axis_size(axis))
    route = [(i - distance, i) for i in devices if i - distance in devices]
    return lax.ppermute(block, axis, route)


def front(inputs, gain_vector):
    return (
        inputs
        * lax.rsqrt(jnp.mean(inputs * inputs, axis=-1, keepdims=True) + epsilon)
        * gain_vector
    )


def gated_norm(mixed_values, gate_raw, gain_vector):
    gated_values = mixed_values * jax.nn.silu(gate_raw)
    return (
        gated_values
        * lax.rsqrt(jnp.mean(gated_values * gated_values, axis=-1, keepdims=True) + epsilon)
        * gain_vector
    )


def convolve(extended, kernel, offset_bias):
    tap_count = kernel.shape[0]
    rows_out = extended.shape[0] - tap_count + 1
    summed = jnp.broadcast_to(offset_bias[None, :], (rows_out, extended.shape[1]))
    for shift_index in range(tap_count):
        summed = (
            summed + kernel[shift_index][None, :] * extended[shift_index : shift_index + rows_out]
        )
    return jax.nn.silu(summed)


def block_step(carried, pieces, decay_rate, skip_gain):
    block_x, block_dt, block_b, block_c = pieces
    positions = block_dt.shape[0]
    cumulative = jnp.cumsum(block_dt * decay_rate[None, :], axis=0).T
    causal = jnp.arange(positions)[:, None] >= jnp.arange(positions)[None, :]
    spread_gap = cumulative[:, :, None] - cumulative[:, None, :]
    decays = jnp.where(causal[None], jnp.exp(jnp.where(causal[None], spread_gap, 0.0)), 0.0)
    scores = jnp.dot(block_c, block_b.T, precision=highest)
    mixing = scores[None] * decays * block_dt.T[:, None, :]
    heads_x = jnp.transpose(block_x, (1, 0, 2))
    in_block = jnp.einsum("hts,hsp->htp", mixing, heads_x, precision=highest)
    from_state = (
        jnp.einsum("tn,hnp->htp", block_c, carried, precision=highest)
        * jnp.exp(cumulative)[:, :, None]
    )
    outputs = in_block + from_state + skip_gain[:, None, None] * heads_x
    final_sum = cumulative[:, -1]
    weights_in = jnp.exp(final_sum[:, None] - cumulative) * block_dt.T
    updated = carried * jnp.exp(final_sum)[:, None, None] + jnp.einsum(
        "sn,hsp->hnp", block_b, heads_x * weights_in[:, :, None], precision=highest
    )
    return (updated, jnp.transpose(outputs, (1, 0, 2)))


def state_space(mixer_x, dt_raw, both_bc, dt_offset, log_rates, skip_gain):
    length_all = mixer_x.shape[0]
    head_count = dt_raw.shape[1]
    head_width = mixer_x.shape[1] // head_count
    state_width = both_bc.shape[1] // 2
    blocks = length_all // BLOCK
    step_dt = jax.nn.softplus(dt_raw + dt_offset[None, :])
    decay_rate = -jnp.exp(log_rates)
    scanned = (
        mixer_x.reshape(blocks, BLOCK, head_count, head_width),
        step_dt.reshape(blocks, BLOCK, head_count),
        both_bc[:, :state_width].reshape(blocks, BLOCK, state_width),
        both_bc[:, state_width:].reshape(blocks, BLOCK, state_width),
    )
    stepper = jax.checkpoint(partial(block_step, decay_rate=decay_rate, skip_gain=skip_gain))
    initial = jnp.zeros((head_count, state_width, head_width), mixer_x.dtype)
    _, outputs = lax.scan(stepper, initial, scanned)
    return outputs.reshape(length_all, head_count * head_width)


def per_device(
    tokens,
    norm_gain,
    in_proj,
    conv_weight,
    conv_bias,
    dt_bias,
    a_log,
    skip_d,
    gate_norm,
    out_proj,
    cotangent,
):
    inner_width = gate_norm.shape[0]
    channels = conv_bias.shape[0]
    tap_count = conv_weight.shape[0]
    head_total = dt_bias.shape[0]
    contract_rows = (((0,), (0,)), ((), ()))
    contract_cols = (((1,), (1,)), ((), ()))
    in_full, out_full = (
        lax.all_gather(in_proj, "dp", axis=0, tiled=True),
        lax.all_gather(out_proj, "dp", axis=0, tiled=True),
    )
    inputs = tokens.astype(jnp.float32)
    normed, front_back = jax.vjp(front, inputs, norm_gain)
    normed_low = normed.astype(jnp.bfloat16)
    projected = jnp.dot(normed_low, in_full, preferred_element_type=jnp.float32).astype(
        jnp.bfloat16
    )
    gate_raw = projected[:, :inner_width]
    conv_in = projected[:, inner_width : inner_width + channels]
    dt_raw = projected[:, inner_width + channels :]
    rows_here = conv_in.shape[0]
    edge_rows = passed_along(conv_in[rows_here - (tap_count - 1) :], "seq", 1)
    extended = jnp.concatenate([edge_rows, conv_in], axis=0).astype(jnp.float32)
    activated, conv_back = jax.vjp(convolve, extended, conv_weight, conv_bias)
    mixer_x = activated[:, :inner_width].astype(jnp.bfloat16)
    both_bc = activated[:, inner_width:].astype(jnp.bfloat16)
    heads_x, heads_dt = (
        lax.all_to_all(mixer_x, "seq", split_axis=1, concat_axis=0, tiled=True),
        lax.all_to_all(dt_raw, "seq", split_axis=1, concat_axis=0, tiled=True),
    )
    whole_bc = lax.all_gather(both_bc, "seq", axis=0, tiled=True)
    local_heads = heads_dt.shape[1]
    first_head = lax.axis_index("seq") * local_heads
    local_offset = lax.dynamic_slice_in_dim(dt_bias, first_head, local_heads)
    local_alog = lax.dynamic_slice_in_dim(a_log, first_head, local_heads)
    local_skip = lax.dynamic_slice_in_dim(skip_d, first_head, local_heads)
    mixed_heads, mixer_back = jax.vjp(
        state_space,
        heads_x.astype(jnp.float32),
        heads_dt.astype(jnp.float32),
        whole_bc.astype(jnp.float32),
        local_offset,
        local_alog,
        local_skip,
    )
    mixed_tok = lax.all_to_all(
        mixed_heads.astype(jnp.bfloat16), "seq", split_axis=0, concat_axis=1, tiled=True
    )
    branch_in, tail_back = jax.vjp(
        gated_norm, mixed_tok.astype(jnp.float32), gate_raw.astype(jnp.float32), gate_norm
    )
    branch_low = branch_in.astype(jnp.bfloat16)
    block_out = (inputs + jnp.dot(branch_low, out_full, preferred_element_type=jnp.float32)).astype(
        jnp.bfloat16
    )
    grad_out_w = lax.dot_general(
        branch_low, cotangent, contract_rows, preferred_element_type=jnp.float32
    )
    grad_branch = lax.dot_general(
        cotangent, out_full, contract_cols, preferred_element_type=jnp.float32
    )
    grad_mixed, grad_gate_raw, grad_gate_norm = tail_back(grad_branch)
    grad_heads = lax.all_to_all(
        grad_mixed.astype(jnp.bfloat16), "seq", split_axis=1, concat_axis=0, tiled=True
    )
    grad_x, grad_dt, grad_bc, grad_offset, grad_alog, grad_skip = mixer_back(
        grad_heads.astype(jnp.float32)
    )
    back_x, back_dt = (
        lax.all_to_all(grad_x.astype(jnp.bfloat16), "seq", split_axis=0, concat_axis=1, tiled=True),
        lax.all_to_all(
            grad_dt.astype(jnp.bfloat16), "seq", split_axis=0, concat_axis=1, tiled=True
        ),
    )
    local_bc = lax.psum_scatter(grad_bc, "seq", scatter_dimension=0, tiled=True)
    grad_act = jnp.concatenate([back_x.astype(jnp.float32), local_bc], axis=1)
    grad_ext, grad_kernel, grad_cbias = conv_back(grad_act)
    edge_grad = passed_along(grad_ext[: tap_count - 1], "seq", -1)
    grad_conv_in = grad_ext[tap_count - 1 :] + jnp.concatenate(
        [jnp.zeros((rows_here - (tap_count - 1), channels), jnp.float32), edge_grad], axis=0
    )
    grad_proj = jnp.concatenate(
        [grad_gate_raw, grad_conv_in, back_dt.astype(jnp.float32)], axis=1
    ).astype(jnp.bfloat16)
    grad_in_w = lax.dot_general(
        normed_low, grad_proj, contract_rows, preferred_element_type=jnp.float32
    )
    grad_normed = lax.dot_general(
        grad_proj, in_full, contract_cols, preferred_element_type=jnp.float32
    )
    grad_inputs, grad_gain = front_back(grad_normed)
    input_grad = (cotangent.astype(jnp.float32) + grad_inputs).astype(jnp.bfloat16)
    part_in, part_out = (
        lax.psum_scatter(grad_in_w, "seq", scatter_dimension=1, tiled=True),
        lax.psum_scatter(grad_out_w, "seq", scatter_dimension=1, tiled=True),
    )
    in_proj_grad, out_proj_grad = (
        lax.psum_scatter(part_in, "dp", scatter_dimension=0, tiled=True),
        lax.psum_scatter(part_out, "dp", scatter_dimension=0, tiled=True),
    )
    zero_heads = jnp.zeros((head_total,), jnp.float32)
    full_offset = lax.dynamic_update_slice_in_dim(zero_heads, grad_offset, first_head, 0)
    full_alog = lax.dynamic_update_slice_in_dim(zero_heads, grad_alog, first_head, 0)
    full_skip = lax.dynamic_update_slice_in_dim(zero_heads, grad_skip, first_head, 0)
    small_sums = lax.psum(
        (grad_gain, grad_kernel, grad_cbias, full_offset, full_alog, full_skip, grad_gate_norm),
        ("dp", "seq"),
    )
    return (
        block_out,
        input_grad,
        small_sums[0],
        in_proj_grad,
        small_sums[1],
        small_sums[2],
        small_sums[3],
        small_sums[4],
        small_sums[5],
        small_sums[6],
        out_proj_grad,
    )


def solution(mesh):
    in_specs = (
        P(("dp", "seq"), None),
        P(),
        P("dp", None),
        P(),
        P(),
        P(),
        P(),
        P(),
        P(),
        P("dp", None),
        P(("dp", "seq"), None),
    )
    out_specs = (
        P(("dp", "seq"), None),
        P(("dp", "seq"), None),
        P(),
        P("dp", "seq"),
        P(),
        P(),
        P(),
        P(),
        P(),
        P(),
        P("dp", "seq"),
    )
    return jax.shard_map(
        per_device, mesh=mesh, in_specs=in_specs, out_specs=out_specs, check_vma=False
    )
```

profile of v0, /device:TPU:0, one launch (start us, length us, event | category | flops | bytes accessed | tf_op | source)
XLA Modules:
  0.0 1854.0 jit_solution(7094472910029923175)
XLA Ops:
  11.7 59.5 %all-gather.4.cloned.1.call-done = bf16[1024,4384]{0,1:T(8,128)(2,1)} async-done(((bf16[128,4384]{0,1:T(8,128)(2,1)}), bf16[1024,4384]{0,1:T(8,128)(2,1)}) %all-gather.4.cloned.1.call-update) | async-done | bytes 8978448 | tf_op jit(solution)/shard_map/all_gather | solution.py:113
  71.2 12.9 convolution_convert_fusion
  106.9 11.8 multiply_convert_fusion
  131.7 76.2 %all-gather.6.cloned.1.call-done = bf16[4096,256]{0,1:T(8,128)(2,1)} async-done(((bf16[1024,256]{0,1:T(8,128)(2,1)}), bf16[4096,256]{0,1:T(8,128)(2,1)}) %all-gather.6.cloned.1.call-update) | async-done | bytes 2097168 | tf_op jit(solution)/shard_map/all_gather | solution.py:135
  215.9 39.4 %all-to-all-done.1 = bf16[1024,4,512]{0,2,1:T(8,128)(2,1)} async-done(((bf16[1024,4,512]{0,2,1:T(8,128)(2,1)}), bf16[1024,4,512]{0,2,1:T(8,128)(2,1)}, u32[]{:S(2)}, u32[]{:S(2)}) %all-to-all-start.1) | async-done | bytes 4194336 | tf_op jit(solution)/shard_map/all_to_all | solution.py:132
  261.9 12.0 copy.88
  273.9 10.9 reshape.442
  284.8 11.5 copy.89
  298.9 178.0 %while.46 = (s32[]{:T(128)}, f32[8,128,64]{1,2,0:T(8,128)S(1)}, bf16[16,256,8,64]{1,3,2,0:T(8,128)(2,1)}, f32[16,8,128,64]{2,3,1,0:T(8,128)}, f32[16,256,8]{1,2,...) while((s32[]{:T(128)}, f32[8,128,64]{1,2,0:T(8,128)S(1)}, ...), condition=%wide.region_4.5_spmd.clone.clone, body=%wide.region_1.4_spmd.clone.clone.sunk | while | flops 909711360 | bytes 5969247 | solution.py:89
  476.9 6.8 copy.92
  483.8 7.2 convert_element_type.126
  502.1 92.0 %all-to-all-done.2 = bf16[4,1024,512]{1,2,0:T(8,128)(2,1)} async-done(((bf16[4,1024,512]{1,2,0:T(8,128)(2,1)}), bf16[4,1024,512]{1,2,0:T(8,128)(2,1)}, u32[]{:S(2)}, u32[]{:S(2)}) %all-to-all-start.2) | async-done | bytes 4194336 | tf_op jit(solution)/shard_map/all_to_all | solution.py:150
  594.1 7.5 multiply_reduce_fusion.9
  601.6 12.0 multiply_reduce_fusion.7
  613.7 10.5 fusion.113
  629.5 92.3 %all-to-all-done.3 = bf16[1024,4,512]{0,2,1:T(8,128)(2,1)} async-done(((bf16[1024,4,512]{0,2,1:T(8,128)(2,1)}), bf16[1024,4,512]{0,2,1:T(8,128)(2,1)}, u32[]{:S(2)}, u32[]{:S(2)}) %all-to-all-start.3) | async-done | bytes 4194336 | tf_op jit(solution)/shard_map/all_to_all | solution.py:167
  728.4 12.0 copy.95
  740.4 10.7 reshape.444
  756.7 371.8 %while.45 = (s32[]{:T(128)}, f32[8]{0:T(128)S(1)}, f32[8]{0:T(128)S(1)}, f32[8,128,64]{1,2,0:T(8,128)S(1)}, bf16[16,256,8,64]{1,3,2,0:T(8,128)(2,1)}, /*index=5*...) while((s32[]{:T(128)}, f32[8]{0:T(128)S(1)}, ...), condition=%wide.region_22.23_spmd.clone, body=%wide.region_7.22_spmd.clone.sunk | while | flops 2127069184 | bytes 17461760 | solution.py:89
  1138.3 10.7 fusion.144
  1155.7 7.2 convert_element_type.139
  1174.5 158.8 %all-to-all-done.4 = bf16[4,1024,512]{1,2,0:T(8,128)(2,1)} async-done(((bf16[4,1024,512]{1,2,0:T(8,128)(2,1)}), bf16[4,1024,512]{1,2,0:T(8,128)(2,1)}, u32[]{:S(2)}, u32[]{:S(2)}) %all-to-all-start.4) | async-done | bytes 4194336 | tf_op jit(solution)/shard_map/all_to_all | solution.py:174
  1343.2 27.6 %multiply_reduce_fusion.6 = (f32[2304]{0:T(1024)S(1)}, f32[2304]{0:T(1024)S(1)}, f32[2304]{0:T(1024)S(1)}, f32[2304]{0:T(1024)S(1)}, f32[2304]{0:T(1024)S(1)}, /*index=5*/f32[1024,2304]{0,1:T(8,128)}) fusion(f32[1027,2304]{0,1:T(8,128)} %copy-done, f32[1024,2304]{0,1:T(8,128)} %get-tuple-element.806, f32[1024,256]{0,1:T(8,128)} %reduce-scatter.6.cloned.1.call-done, ...), kind=kLoop, calls=%fused_computation.152 | loop fusion | flops 44815104 | bytes 66106368 | tf_op jit(solution)/shard_map/transpose(jvp())/reduce_sum | solution.py:44
  1370.8 10.7 broadcast_multiply_fusion
  1392.0 19.6 %pad_add_fusion = f32[1027,2304]{0,1:T(8,128)} fusion(f32[1024,2304]{0,1:T(8,128)} %copy-done.2, f32[1024,2304]{0,1:T(8,128)} %get-tuple-element.817, f32[1024,2304]{0,1:T(8,128)} %get-tuple-element.818, f32[1024,2304]{0,1:T(8,128)} %copy-done.1), kind=kLoop, calls=%fused_computation.142 | loop fusion | flops 7098624 | bytes 47213568 | tf_op jit(solution)/shard_map/transpose(jvp())/add_any | solution.py:44
  1412.1 8.5 fusion.107
  1420.6 19.5 %fusion.123 = f32[1024,4384]{0,1:T(8,128)} fusion(bf16[1024,32]{0,1:T(8,128)(2,1)S(1)} %bitcast.414, bf16[1024,2304]{0,1:T(8,128)(2,1)} %fusion.107, bf16[1024,2048]{0,1:T(8,128)(2,1)} %get-tuple-element.813, bf16[1024,1024]{1,0:T(8,128)(2,1)S(1)} %copy-done.6, f32[1024]{0:T(1024)} %param.16, f32[1024]{0:T(1024)S(1)} %copy-done.23), kind=kOutput, calls=%fused_computation.193 | convolution fusion | flops 9225043968 | bytes 29040640 | tf_op jit(solution)/shard_map/dot_general | solution.py:189
  1441.2 300.5 %reduce-scatter.8.cloned.1.call-done = f32[1024,1096]{0,1:T(8,128)} async-done(((f32[1024,4384]{0,1:T(8,128)}), f32[1024,1096]{0,1:T(8,128)}) %reduce-scatter.8.cloned.1.call-update) | async-done | bytes 4489232 | tf_op jit(solution)/shard_map/reduce_scatter | solution.py:198
  1741.7 10.8 fusion.121
  1753.6 17.5 fusion.117
  1771.1 42.4 %all-reduce.12 = (f32[1024]{0:T(1024)}, f32[4,2304]{1,0:T(4,128)}, f32[2304]{0:T(1024)}, f32[32]{0:T(128)}, f32[32]{0:T(128)}, /*index=5*/f32[32]{0:T(128)}, f32[2048]{0:T(1024)}) all-reduce(f32[1024]{0:T(1024)S(1)} %get-tuple-element.725, f32[4,2304]{1,0:T(4,128)S(1)} %pad_add_fusion.3, ...), channel_id=1, replica_groups=mesh['dp'=8,'seq'=4] {'dp','seq'}, use_global_device_ids=true, to_apply=%region_26.27 | all-reduce | flops 14688 | bytes 117504 | tf_op jit(solution)/shard_map/psum | solution.py:209
  1818.7 28.2 %reduce-scatter.10.cloned.1.call-done = f32[128,1096]{0,1:T(8,128)} async-done(((f32[1024,1096]{0,1:T(8,128)}), f32[128,1096]{0,1:T(8,128)}) %reduce-scatter.10.cloned.1.call-update) | async-done | bytes 561168 | tf_op jit(solution)/shard_map/reduce_scatter | solution.py:202
  (1016 shorter events, 688.6 us)
Async XLA Ops:
  7.2 64.0 %all-gather.4.cloned.1.call-start = ((), (), s32[]{:S(2)}) async-start(), calls=%async_computation.11 | async-start | bytes 10100736 | tf_op jit(solution)/shard_map/all_gather | solution.py:113
  9.0 97.9 %copy-start.12 = (f32[2304]{0:T(1024)}, f32[2304]{0:T(1024)S(1)}, u32[]{:S(2)}) copy-start(f32[2304]{0:T(1024)S(1)} %get-tuple-element.727) | copy-start | bytes 27652
  9.0 97.9 %copy-start.14 = (f32[2304]{0:T(1024)}, f32[2304]{0:T(1024)S(1)}, u32[]{:S(2)}) copy-start(f32[2304]{0:T(1024)S(1)} %get-tuple-element.728) | copy-start | bytes 27652
  9.0 97.9 %copy-start.16 = (f32[2304]{0:T(1024)}, f32[2304]{0:T(1024)S(1)}, u32[]{:S(2)}) copy-start(f32[2304]{0:T(1024)S(1)} %get-tuple-element.729) | copy-start | bytes 27652
  9.0 97.9 %copy-start.18 = (f32[2304]{0:T(1024)}, f32[2304]{0:T(1024)S(1)}, u32[]{:S(2)}) copy-start(f32[2304]{0:T(1024)S(1)} %get-tuple-element.730) | copy-start | bytes 27652
  11.7 59.5 %copy-start.22 = (f32[1024]{0:T(1024)}, f32[1024]{0:T(1024)S(1)}, u32[]{:S(2)}) copy-start(f32[1024]{0:T(1024)S(1)} %fusion.139) | copy-start | bytes 12292
  88.1 13.5 collective-permute-start
  97.9 25.4 %all-to-all-start = ((bf16[1024,4,8]{0,2,1:T(8,128)(2,1)}), bf16[1024,4,8]{0,2,1:T(8,128)(2,1)S(1)}, u32[]{:S(2)}, u32[]{:S(2)}) async-start(bf16[1024,4,8]{0,2,1:T(8,128)(2,1)} %slice_bitcast_fusion), calls=%async_computation | async-start | bytes 131072 | tf_op jit(solution)/shard_map/all_to_all | solution.py:133
  123.3 132.1 %all-to-all-start.1 = ((bf16[1024,4,512]{0,2,1:T(8,128)(2,1)}), bf16[1024,4,512]{0,2,1:T(8,128)(2,1)}, u32[]{:S(2)}, u32[]{:S(2)}) async-start(bf16[1024,4,512]{0,2,1:T(8,128)(2,1)} %bitcast.401), calls=%async_computation.1 | async-start | bytes 8388608 | tf_op jit(solution)/shard_map/all_to_all | solution.py:132
  128.5 79.4 %all-gather.6.cloned.1.call-start = ((), (), s32[]{:S(2)}) async-start(), calls=%async_computation.12 | async-start | bytes 2621440 | tf_op jit(solution)/shard_map/all_gather | solution.py:135
  130.7 83.4 %copy-start.28 = (f32[8]{0:T(128)}, f32[8]{0:T(128)S(1)}, u32[]{:S(2)}) copy-start(f32[8]{0:T(128)S(1)} %dynamic_slice.91) | copy-start | bytes 100
  496.5 97.6 %all-to-all-start.2 = ((bf16[4,1024,512]{1,2,0:T(8,128)(2,1)}), bf16[4,1024,512]{1,2,0:T(8,128)(2,1)}, u32[]{:S(2)}, u32[]{:S(2)}) async-start(bf16[4,1024,512]{1,2,0:T(8,128)(2,1)} %copy.93), calls=%async_computation.2 | async-start | bytes 8388608 | tf_op jit(solution)/shard_map/all_to_all | solution.py:150
  501.4 100.2 %all-gather.8.cloned.1.call-start = ((), (), s32[]{:S(2)}) async-start(), calls=%async_computation.13 | async-start | bytes 4718592 | tf_op jit(solution)/shard_map/all_gather | solution.py:114
  502.1 99.5 %copy-start.26 = (f32[2048]{0:T(1024)S(1)}, f32[2048]{0:T(1024)}, u32[]{:S(2)}) copy-start(f32[2048]{0:T(1024)} %param.23) | copy-start | bytes 24580
  601.6 12.1 slice-start
  601.6 12.1 slice-start.1
  624.2 97.5 %all-to-all-start.3 = ((bf16[1024,4,512]{0,2,1:T(8,128)(2,1)}), bf16[1024,4,512]{0,2,1:T(8,128)(2,1)}, u32[]{:S(2)}, u32[]{:S(2)}) async-start(bf16[1024,4,512]{0,2,1:T(8,128)(2,1)} %bitcast.402), calls=%async_computation.3 | async-start | bytes 8388608 | tf_op jit(solution)/shard_map/all_to_all | solution.py:167
  629.1 714.1 %reduce-scatter.6.cloned.1.call-start = ((), (), s32[]{:S(2)}) async-start(), calls=%async_computation.14 | async-start | bytes 5242880 | tf_op jit(solution)/shard_map/reduce_scatter | solution.py:179
  1138.3 302.5 %reduce-scatter.12.cloned.1.call-start = ((), (), s32[]{:S(2)}) async-start(), calls=%async_computation.17 | async-start | bytes 10485760 | tf_op jit(solution)/shard_map/reduce_scatter | solution.py:199
  1168.6 164.6 %all-to-all-start.4 = ((bf16[4,1024,512]{1,2,0:T(8,128)(2,1)}), bf16[4,1024,512]{1,2,0:T(8,128)(2,1)}, u32[]{:S(2)}, u32[]{:S(2)}) async-start(bf16[4,1024,512]{1,2,0:T(8,128)(2,1)} %copy.101), calls=%async_computation.4 | async-start | bytes 8388608 | tf_op jit(solution)/shard_map/all_to_all | solution.py:174
  1333.2 87.4 %all-to-all-start.5 = ((bf16[4,1024,8]{1,2,0:T(8,128)(2,1)}), bf16[4,1024,8]{1,2,0:T(8,128)(2,1)S(1)}, u32[]{:S(2)}, u32[]{:S(2)}) async-start(bf16[4,1024,8]{1,2,0:T(8,128)(2,1)} %fusion.130), calls=%async_computation.6 | async-start | bytes 131072 | tf_op jit(solution)/shard_map/all_to_all | solution.py:175
  1336.5 405.1 %reduce-scatter.8.cloned.1.call-start = ((), (), s32[]{:S(2)}) async-start(), calls=%async_computation.15 | async-start | bytes 22446080 | tf_op jit(solution)/shard_map/reduce_scatter | solution.py:198
  1343.2 27.6 %copy-start.13 = (f32[2304]{0:T(1024)S(1)}, f32[2304]{0:T(1024)}, u32[]{:S(2)}) copy-start(f32[2304]{0:T(1024)} %copy-done.12) | copy-start | bytes 27652
  1343.2 27.6 %copy-start.15 = (f32[2304]{0:T(1024)S(1)}, f32[2304]{0:T(1024)}, u32[]{:S(2)}) copy-start(f32[2304]{0:T(1024)} %copy-done.14) | copy-start | bytes 27652
  1343.2 27.6 %copy-start.17 = (f32[2304]{0:T(1024)S(1)}, f32[2304]{0:T(1024)}, u32[]{:S(2)}) copy-start(f32[2304]{0:T(1024)} %copy-done.16) | copy-start | bytes 27652
  1343.2 27.6 %copy-start.19 = (f32[2304]{0:T(1024)S(1)}, f32[2304]{0:T(1024)}, u32[]{:S(2)}) copy-start(f32[2304]{0:T(1024)} %copy-done.18) | copy-start | bytes 27652
  1390.7 20.9 %collective-permute-start.1 = (f32[3,2304]{1,0:T(4,128)S(1)}, f32[3,2304]{1,0:T(4,128)S(1)}, u32[]{:S(2)}, u32[]{:S(2)}) collective-permute-start(f32[3,2304]{1,0:T(4,128)S(1)} %copy.104), channel_id=1, source_target_pairs={{1,0},{2,1},{3,2},{5,4},{6,5},{7,6},{9,8},{10,9},{11,10},{13,12},{... | collective-permute-start | bytes 82952 | tf_op jit(solution)/shard_map/ppermute | solution.py:18
  1440.2 301.5 %copy-start.27 = (f32[2048]{0:T(1024)S(1)}, f32[2048]{0:T(1024)}, u32[]{:S(2)}) copy-start(f32[2048]{0:T(1024)} %param.23) | copy-start | bytes 24580
  1440.2 378.6 %reduce-scatter.14.cloned.1.call-start = ((), (), s32[]{:S(2)}) async-start(), calls=%async_computation.18 | async-start | bytes 2359296 | tf_op jit(solution)/shard_map/reduce_scatter | solution.py:203
  1440.9 406.1 %reduce-scatter.10.cloned.1.call-start = ((), (), s32[]{:S(2)}) async-start(), calls=%async_computation.16 | async-start | bytes 5050368 | tf_op jit(solution)/shard_map/reduce_scatter | solution.py:202
  1753.6 17.5 copy-start.25
  1753.6 60.0 %copy-start.21 = (f32[1024]{0:T(1024)S(1)}, f32[1024]{0:T(1024)}, u32[]{:S(2)}) copy-start(f32[1024]{0:T(1024)} %copy-done.20) | copy-start | bytes 12292
  (21 other events, 133.1 us)
Sparse Core Ops, SparseCore 0:
  9.9 61.2 all-gather.3
  131.5 76.3 all-gather.5
  504.1 37.1 all-gather.7
  1138.4 114.8 reduce-scatter.5
  1255.6 185.1 reduce-scatter.11
  1443.1 298.5 reduce-scatter.7
  1745.9 42.2 reduce-scatter.13
  1792.2 54.7 reduce-scatter.9
where the time goes:
time: 1870 us; the launch traced here: 1850 us
  waiting for transfers between devices  849 us (45%)
  matrix products  433 us (23%)
  local copies, waits for them, and re-layouts  251 us (13%)
  other arithmetic  228 us (12%)
  blocking collectives  42.4 us (2%)
  starting transfers between devices  32.4 us (2%)
    reduce_scatter x1, waiting for transfers between devices, per_device(): lax.psum_scatter(grad_in_w, 'seq', scatter_dimension=1, tiled=True)  300 us
    dot_general x48, matrix products, block_step(): in_block = jnp.einsum('hts,hsp->htp', mixing, heads_x, precision=highest)  175 us
    all_to_all x1, waiting for transfers between devices, per_device(): lax.all_to_all(grad_x.astype(jnp.bfloat16), 'seq', split_axis=0, concat_a...  159 us
    another operation x147, other arithmetic  94.1 us
    all_to_all x1, waiting for transfers between devices, per_device(): lax.all_to_all(grad_mixed.astype(jnp.bfloat16), 'seq', split_axis=1, conc...  92.3 us
    all_to_all x1, waiting for transfers between devices, per_device(): lax.all_to_all(mixed_heads.astype(jnp.bfloat16), 'seq', split_axis=0, con...  92 us
    all_gather x1, waiting for transfers between devices, per_device(): whole_bc = lax.all_gather(both_bc, 'seq', axis=0, tiled=True)  76.2 us
    dot_general x64, matrix products, block_step(): scores = jnp.dot(block_c, block_b.T, precision=highest)  64.1 us
  transfers between devices with their start and end apart: 16, of which 9 were waited for; matrix products, arithmetic and copies ran while one was open for 11% of the time, Pallas kernels for 0%

commit v1 on v0

v1 whole, which is shorter than its diff:
```python
import jax
import jax.numpy as jnp
from jax import lax
from jax.sharding import PartitionSpec as P

BLOCK = 128


epsilon = 1e-05
highest = lax.Precision.HIGHEST


def passed_along(block, axis, distance):
    devices = range(lax.axis_size(axis))
    route = [(i - distance, i) for i in devices if i - distance in devices]
    return lax.ppermute(block, axis, route)


def front(inputs, gain_vector):
    return (
        inputs
        * lax.rsqrt(jnp.mean(inputs * inputs, axis=-1, keepdims=True) + epsilon)
        * gain_vector
    )


def gated_norm(mixed_values, gate_raw, gain_vector):
    gated_values = mixed_values * jax.nn.silu(gate_raw)
    return (
        gated_values
        * lax.rsqrt(jnp.mean(gated_values * gated_values, axis=-1, keepdims=True) + epsilon)
        * gain_vector
    )


def convolve(extended, kernel, offset_bias):
    tap_count = kernel.shape[0]
    rows_out = extended.shape[0] - tap_count + 1
    summed = jnp.broadcast_to(offset_bias[None, :], (rows_out, extended.shape[1]))
    for shift_index in range(tap_count):
        summed = (
            summed + kernel[shift_index][None, :] * extended[shift_index : shift_index + rows_out]
        )
    return jax.nn.silu(summed)


def chained(finals, decays):
    carried = jnp.zeros_like(finals[0])
    befores = []
    for index in range(finals.shape[0]):
        befores.append(carried)
        carried = carried * decays[index][None, :, None] + finals[index]
    return jnp.stack(befores)


@jax.custom_vjp
def entering_state(final, decay):
    return entering_keep(final, decay)[0]


def entering_keep(final, decay):
    finals = lax.all_gather(final.astype(jnp.bfloat16), "seq").astype(jnp.float32)
    decays = lax.all_gather(decay, "seq")
    befores = chained(finals, decays)
    here = lax.axis_index("seq")
    return lax.dynamic_index_in_dim(befores, here, 0, keepdims=False), (finals, decays)


def entering_back(kept, grad):
    grads = lax.all_gather(grad.astype(jnp.bfloat16), "seq").astype(jnp.float32)
    _, pull = jax.vjp(chained, *kept)
    here = lax.axis_index("seq")
    return tuple(lax.dynamic_index_in_dim(g, here, 0, keepdims=False) for g in pull(grads))


entering_state.defvjp(entering_keep, entering_back)


def state_space(mixer_x, dt_raw, both_bc, dt_offset, log_rates, skip_gain):
    low = jnp.bfloat16
    rows = mixer_x.shape[0]
    heads = dt_raw.shape[1]
    width = mixer_x.shape[1] // heads
    states = both_bc.shape[1] // 2
    blocks = rows // BLOCK
    step_dt = jax.nn.softplus(dt_raw + dt_offset[None, :]).reshape(blocks, BLOCK, heads)
    decay_rate = -jnp.exp(log_rates)
    causal = jnp.arange(BLOCK)[:, None] >= jnp.arange(BLOCK)[None, :]
    cumulative = jnp.einsum(
        "ts,bsh->bht", causal.astype(jnp.float32), step_dt * decay_rate, precision=highest
    )
    steps = jnp.transpose(step_dt, (0, 2, 1))
    block_b = both_bc[:, :states].reshape(blocks, BLOCK, states).astype(low)
    block_c = both_bc[:, states:].reshape(blocks, BLOCK, states).astype(low)
    block_x = mixer_x.reshape(blocks, BLOCK, heads, width)
    spread_gap = cumulative[:, :, :, None] - cumulative[:, :, None, :]
    decays = jnp.where(causal, jnp.exp(jnp.where(causal, spread_gap, 0.0)), 0.0)
    scores = jnp.einsum("btn,bsn->bts", block_c, block_b, preferred_element_type=jnp.float32)
    mixing = scores[:, None] * decays * steps[:, :, None, :]
    in_block = jnp.einsum(
        "bhts,bshp->bthp", mixing.astype(low), block_x.astype(low),
        preferred_element_type=jnp.float32,
    )
    final_sum = cumulative[:, :, -1]
    weights_in = jnp.transpose(jnp.exp(final_sum[:, :, None] - cumulative) * steps, (0, 2, 1))
    weighted = (block_x * weights_in[..., None]).astype(low).reshape(blocks, BLOCK, heads * width)
    added = jnp.einsum("bsn,bsc->bnc", block_b, weighted, preferred_element_type=jnp.float32)
    added = added.reshape(blocks, states, heads, width)
    block_decay = jnp.exp(final_sum)
    local = chained(added, block_decay)
    final = local[-1] * block_decay[-1][None, :, None] + added[-1]
    entered = entering_state(final, jnp.exp(jnp.sum(final_sum, axis=0)))
    reach = jnp.exp(jnp.cumsum(final_sum, axis=0) - final_sum)
    carried = local + reach[:, None, :, None] * entered[None]
    from_state = jnp.einsum(
        "btn,bnc->btc", block_c, carried.astype(low).reshape(blocks, states, heads * width),
        preferred_element_type=jnp.float32,
    ).reshape(blocks, BLOCK, heads, width)
    outputs = (
        in_block
        + from_state * jnp.exp(jnp.transpose(cumulative, (0, 2, 1)))[..., None]
        + skip_gain[:, None] * block_x
    )
    return outputs.reshape(rows, heads * width)


def per_device(
    tokens,
    norm_gain,
    in_proj,
    conv_weight,
    conv_bias,
    dt_bias,
    a_log,
    skip_d,
    gate_norm,
    out_proj,
    cotangent,
):
    inner_width = gate_norm.shape[0]
    channels = conv_bias.shape[0]
    tap_count = conv_weight.shape[0]
    contract_rows = (((0,), (0,)), ((), ()))
    contract_cols = (((1,), (1,)), ((), ()))
    in_rest = lax.all_gather(in_proj[:, inner_width:], "dp", axis=0, tiled=True)
    gate_rows, out_rows, in_rest = lax.optimization_barrier(
        (in_proj[:, :inner_width], out_proj, in_rest)
    )
    in_gate = lax.all_gather(gate_rows, "dp", axis=0, tiled=True)
    out_full = lax.all_gather(out_rows, "dp", axis=0, tiled=True)
    inputs = tokens.astype(jnp.float32)
    normed, front_back = jax.vjp(front, inputs, norm_gain)
    normed_low = normed.astype(jnp.bfloat16)
    projected = jnp.dot(normed_low, in_rest, preferred_element_type=jnp.float32).astype(
        jnp.bfloat16
    )
    conv_in = projected[:, :channels]
    dt_raw = projected[:, channels:]
    rows_here = conv_in.shape[0]
    edge_rows = passed_along(conv_in[rows_here - (tap_count - 1) :], "seq", 1)
    extended = jnp.concatenate([edge_rows, conv_in], axis=0).astype(jnp.float32)
    activated, conv_back = jax.vjp(convolve, extended, conv_weight, conv_bias)
    mixer_x = activated[:, :inner_width].astype(jnp.bfloat16)
    both_bc = activated[:, inner_width:].astype(jnp.bfloat16)
    mixed, mixer_back = jax.vjp(
        state_space,
        mixer_x.astype(jnp.float32),
        dt_raw.astype(jnp.float32),
        both_bc.astype(jnp.float32),
        dt_bias,
        a_log,
        skip_d,
    )
    gate_raw = jnp.dot(normed_low, in_gate, preferred_element_type=jnp.float32).astype(
        jnp.bfloat16
    )
    branch_in, tail_back = jax.vjp(
        gated_norm,
        mixed.astype(jnp.bfloat16).astype(jnp.float32),
        gate_raw.astype(jnp.float32),
        gate_norm,
    )
    branch_low = branch_in.astype(jnp.bfloat16)
    block_out = (inputs + jnp.dot(branch_low, out_full, preferred_element_type=jnp.float32)).astype(
        jnp.bfloat16
    )
    grad_branch = lax.dot_general(
        cotangent, out_full, contract_cols, preferred_element_type=jnp.float32
    )
    grad_mixed, grad_gate_raw, grad_gate_norm = tail_back(grad_branch)
    grad_gate = grad_gate_raw.astype(jnp.bfloat16)
    grad_out_w = lax.dot_general(
        branch_low, cotangent, contract_rows, preferred_element_type=jnp.float32
    ).astype(jnp.bfloat16)
    grad_gate_w = lax.dot_general(
        normed_low, grad_gate, contract_rows, preferred_element_type=jnp.float32
    ).astype(jnp.bfloat16)
    part_out = lax.psum_scatter(grad_out_w, "dp", scatter_dimension=0, tiled=True)
    part_gate = lax.psum_scatter(grad_gate_w, "dp", scatter_dimension=0, tiled=True)
    grad_x, grad_dt, grad_bc, grad_offset, grad_alog, grad_skip = mixer_back(
        grad_mixed.astype(jnp.bfloat16).astype(jnp.float32)
    )
    grad_act = jnp.concatenate(
        [grad_x.astype(jnp.bfloat16).astype(jnp.float32), grad_bc], axis=1
    )
    grad_ext, grad_kernel, grad_cbias = conv_back(grad_act)
    edge_grad = passed_along(grad_ext[: tap_count - 1], "seq", -1)
    grad_conv_in = grad_ext[tap_count - 1 :] + jnp.concatenate(
        [jnp.zeros((rows_here - (tap_count - 1), channels), jnp.float32), edge_grad], axis=0
    )
    grad_rest = jnp.concatenate([grad_conv_in, grad_dt], axis=1).astype(jnp.bfloat16)
    grad_rest_w = lax.dot_general(
        normed_low, grad_rest, contract_rows, preferred_element_type=jnp.float32
    ).astype(jnp.bfloat16)
    grad_rest_w, part_out, part_gate = lax.optimization_barrier((grad_rest_w, part_out, part_gate))
    part_rest = lax.psum_scatter(grad_rest_w, "dp", scatter_dimension=0, tiled=True)
    grad_normed = lax.dot_general(
        grad_gate, in_gate, contract_cols, preferred_element_type=jnp.float32
    ) + lax.dot_general(grad_rest, in_rest, contract_cols, preferred_element_type=jnp.float32)
    grad_inputs, grad_gain = front_back(grad_normed)
    input_grad = (cotangent.astype(jnp.float32) + grad_inputs).astype(jnp.bfloat16)
    part_in = jnp.concatenate([part_gate, part_rest], axis=1).astype(jnp.float32)
    in_proj_grad, out_proj_grad = (
        lax.psum_scatter(part_in, "seq", scatter_dimension=1, tiled=True),
        lax.psum_scatter(part_out.astype(jnp.float32), "seq", scatter_dimension=1, tiled=True),
    )
    smalls = (grad_gain, grad_kernel, grad_cbias, grad_offset, grad_alog, grad_skip, grad_gate_norm)
    joined = lax.psum(jnp.concatenate([v.reshape(-1) for v in smalls]), ("dp", "seq"))
    small_sums, start = [], 0
    for value in smalls:
        small_sums.append(joined[start : start + value.size].reshape(value.shape))
        start += value.size
    return (
        block_out,
        input_grad,
        small_sums[0],
        in_proj_grad,
        *small_sums[1:],
        out_proj_grad,
    )


def solution(mesh):
    in_specs = (
        P(("dp", "seq"), None),
        P(),
        P("dp", None),
        P(),
        P(),
        P(),
        P(),
        P(),
        P(),
        P("dp", None),
        P(("dp", "seq"), None),
    )
    out_specs = (
        P(("dp", "seq"), None),
        P(("dp", "seq"), None),
        P(),
        P("dp", "seq"),
        P(),
        P(),
        P(),
        P(),
        P(),
        P(),
        P("dp", "seq"),
    )
    return jax.shard_map(
        per_device, mesh=mesh, in_specs=in_specs, out_specs=out_specs, check_vma=False
    )
```

time: 1870 us -> 760 us (0.41)
  waiting for transfers between devices: 849 us -> 100 us
  matrix products: 433 us -> 177 us
  local copies, waits for them, and re-layouts: 251 us -> 197 us
  starting transfers between devices: 32.4 us -> 5.52 us
  other arithmetic: 228 us -> 202 us
    all_to_all x6 -> x0, waiting for transfers between devices: 383 us -> none  [the longest x1 159 us: per_device(): lax.all_to_all(grad_x.astype(jnp.bfloat16), 'seq', split_axis=0, concat_a...]
    reduce_scatter x5 -> x2, waiting for transfers between devices: 329 us -> 0.02 us  [the longest x1 0.02 us: per_device(): lax.psum_scatter(grad_out_w, 'dp', scatter_dimension=0, tiled=True)]
    dot_general x211 -> x20, matrix products: 376 us -> 142 us  [the longest x3 47.5 us: state_space(): jnp.einsum('bhts,bshp->bthp', mixing.astype(low), block_x.astype(low), pr...]
    all_gather x3 -> x5, waiting for transfers between devices: 136 us -> 50.5 us  [the longest x1 36.6 us: per_device(): in_rest = lax.all_gather(in_proj[:, inner_width:], 'dp', axis=0, tiled=True)]
    another operation x163 -> x6, other arithmetic: 94.4 us -> 20.4 us
    squeeze x64 -> x0, local copies, waits for them, and re-layouts: 49.7 us -> none  [state_space(): _, outputs = lax.scan(stepper, initial, scanned)]
    unnamed x8 -> x13, waiting for transfers between devices: 1.6 us -> 49.5 us
    convert_element_type x10 -> x5, local copies, waits for them, and re-layouts: 84.8 us -> 41.1 us  [the longest x1 11.2 us: per_device(): grad_x.astype(jnp.bfloat16).astype(jnp.float32)]
  transfers between devices with their start and end apart: 16 -> 12, of which waited for: 9 -> 4; matrix products, arithmetic and copies ran while one was open for 11% -> 56% of each run, Pallas kernels for 0% -> 0%
where the time goes in v1:
time: 760 us; the launch traced here: 753 us
  other arithmetic  202 us (27%)
  local copies, waits for them, and re-layouts  197 us (26%)
  matrix products  177 us (23%)
  waiting for transfers between devices  100 us (13%)
  blocking collectives  53.9 us (7%)
  between operations  16.9 us (2%)
    unnamed x303, local copies, waits for them, and re-layouts  57.1 us
    unnamed x13, waiting for transfers between devices  49.5 us
    dot_general x3, matrix products, state_space(): jnp.einsum('bhts,bshp->bthp', mixing.astype(low), block_x.astype(low), pr...  47.5 us
    psum x1, blocking collectives, per_device(): lax.psum(jnp.concatenate([v.reshape(-1) for v in smalls]), ('dp', 'seq'))  43.8 us
    all_gather x1, waiting for transfers between devices, per_device(): in_rest = lax.all_gather(in_proj[:, inner_width:], 'dp', axis=0, tiled=True)  36.6 us
    reduce_sum x1, other arithmetic, convolve(): kernel[shift_index][None, :] * extended[shift_index:shift_index + rows_out]  27.6 us
    dot_general x3, matrix products, state_space(): jnp.einsum('btn,bnc->btc', block_c, carried.astype(low).reshape(blocks, s...  26 us
    add_any x1, other arithmetic, convolve(): extended[shift_index:shift_index + rows_out]  19.6 us
  transfers between devices with their start and end apart: 12, of which 4 were waited for; matrix products, arithmetic and copies ran while one was open for 56% of the time, Pallas kernels for 0%

profile of v1, /device:TPU:0, one launch (start us, length us, event | category | flops | bytes accessed | tf_op | source)
XLA Modules:
  0.0 752.9 jit_solution(16601037650656179921)
XLA Ops:
  16.6 36.6 %all-gather.7.cloned.1.call-done = bf16[1024,2336]{0,1:T(8,128)(2,1)} async-done(((bf16[128,2336]{0,1:T(8,128)(2,1)}), bf16[1024,2336]{0,1:T(8,128)(2,1)}) %all-gather.7.cloned.1.call-update) | async-done | bytes 4784144 | tf_op jit(solution)/shard_map/all_gather | solution.py:145
  53.2 7.9 %convolution_convert_fusion.2 = bf16[1024,2336]{0,1:T(8,128)(2,1)S(1)} fusion(bf16[1024,2336]{0,1:T(8,128)(2,1)} %all-gather.7.cloned.1.call-done, bf16[1024,1024]{1,0:T(8,128)(2,1)} %param.11, f32[1024]{0:T(1024)} %param.12, f32[1024]{0:T(1024)S(1)} %fusion.120), kind=kOutput, calls=%fused_computation.75 | convolution fusion | flops 4905533440 | bytes 11673600 | tf_op jit(solution)/shard_map/dot_general | solution.py:154
  76.7 9.3 %copy.247 = f32[8,128,2048]{2,1,0:T(8,128)} copy(f32[8,128,2048]{1,2,0:T(8,128)} %bitcast.375) | data formatting | bytes 16777216 | tf_op jit(solution)/shard_map/jvp()/mul | solution.py:106
  91.3 11.9 %multiply_convert_fusion.1 = (bf16[1024,2304]{0,1:T(8,128)(2,1)S(1)}, f32[1024,2304]{0,1:T(8,128)}) fusion(f32[1027,2304]{0,1:T(8,128)S(1)} %maximum_convert_fusion, f32[2304]{0:T(1024)S(1)} %get-tuple-element.52, f32[2304]{0:T(1024)S(1)} %get-tuple-element.53, f32[2304]{0:T(1024)S(1)} %get-tuple-element.51, f32[2304]{0:T(1024)S(1)} %get-tuple-element.50, ...), kind=kLoop, calls=%fused_computation.31 | loop fusion | flops 30670848 | bytes 51950592 | tf_op jit(solution)/shard_map/convert.16
  104.1 7.8 %slice_convert_fusion = (f32[1024,2048]{0,1:T(8,128)}, f32[256,8,8,128]{3,1,2,0:T(8,128)}) fusion(bf16[1024,2304]{0,1:T(8,128)(2,1)S(1)} %get-tuple-element.83), kind=kLoop, calls=%fused_computation.93 | loop fusion | flops 2097152 | bytes 20971520 | tf_op jit(solution)/shard_map/convert_element_type | solution.py:167
  111.9 9.2 %copy.308 = f32[1024,2048]{1,0:T(8,128)} copy(f32[1024,2048]{0,1:T(8,128)} %get-tuple-element.107) | data formatting | bytes 16777216 | tf_op jit(solution)/shard_map/jvp()/reshape | solution.py:95
  168.6 9.2 %copy.266 = f32[8,128,2048]{2,1,0:T(8,128)} copy(f32[8,128,2048]{1,2,0:T(8,128)} %bitcast.376) | data formatting | bytes 16777216 | tf_op jit(solution)/shard_map/jvp()/mul | solution.py:121
  177.9 10.1 %all-reduce.35 = f32[128]{0:T(128)S(1)} all-reduce(f32[128]{0:T(128)S(1)} %exponential_dynamic-update-slice_fusion), channel_id=2, replica_groups=mesh['dp'=8,'seq'=4] {'seq'}, use_global_device_ids=true, to_apply=%add.35 | all-reduce | flops 128 | bytes 1024
  189.9 9.1 %copy.320 = f32[256,8,8,128]{3,2,1,0:T(8,128)} copy(f32[256,8,8,128]{3,1,2,0:T(8,128)} %get-tuple-element.108) | data formatting | bytes 16777216
  225.6 14.4 %fusion.35 = f32[8,128,32,64]{1,3,2,0:T(8,128)S(1)} fusion(f32[8,128,32,64]{1,0,3,2:T(8,128)} %bitcast.377, f32[8,128,32,64]{1,3,2,0:T(8,128)S(1)} %bitcast.380, f32[32]{0:T(128)S(1)} %copy-done.134, f32[8,128,32]{1,2,0:T(8,128)S(1)} %exponential_bitcast_fusion, f32[8,32,128]{2,1,0:T(8,128)S(1)} %copy-done.57, f32[8,32,128]{2,1,0:T(8,128)S(1)} %fusion.99, ...), kind=kOutput, calls=%fused_computation.91 | convolution fusion | flops 576716800 | bytes 26099840 | tf_op jit(solution)/shard_map/jvp(bhts,bshp->bthp)/dot_general | solution.py:100
  240.0 11.0 %copy.261 = f32[8,128,32,64]{1,0,3,2:T(8,128)} copy(f32[8,128,32,64]{1,3,2,0:T(8,128)S(1)} %fusion.35) | data formatting | bytes 16777216 | tf_op jit(solution)/shard_map/convert_element_type | solution.py:179
  251.0 12.7 %multiply_reduce_fusion.10 = (f32[1024]{0:T(1024)S(1)}, f32[1024,2048]{0,1:T(8,128)}, bf16[1024,2048]{0,1:T(8,128)(2,1)}) fusion(f32[256,8,8,128]{3,2,1,0:T(8,128)} %bitcast.383, bf16[1024,2048]{0,1:T(8,128)(2,1)} %all-gather.11.cloned.1.call-done, bf16[1024,1024]{1,0:T(8,128)(2,1)S(1)} %copy-done.27, f32[1024]{0:T(1024)S(1)} %copy-done.120, ...), kind=kOutput, calls=%fused_computation.61 | convolution fusion | flops 4318034944 | bytes 27275264 | tf_op jit(solution)/shard_map/dot_general | solution.py:174
  263.8 13.8 %all-gather.13.cloned.1.call-done = bf16[2048,1024]{1,0:T(8,128)(2,1)} async-done(((bf16[256,1024]{1,0:T(8,128)(2,1)}), bf16[2048,1024]{1,0:T(8,128)(2,1)}) %all-gather.13.cloned.1.call-update) | async-done | bytes 4194320 | tf_op jit(solution)/shard_map/all_gather | solution.py:150
  277.6 14.9 %fusion.21 = (f32[2048]{0:T(1024)}, f32[1024]{0:T(1024)S(1)}, f32[2048,1024]{1,0:T(8,128)}) fusion(f32[1024,2048]{0,1:T(8,128)} %get-tuple-element.71, f32[1024]{0:T(1024)S(1)} %fusion.121, f32[2048]{0:T(1024)} %param.19, bf16[2048,1024]{1,0:T(8,128)(2,1)} %all-gather.13.cloned.1.call-done, bf16[1024,1024]{1,0:T(8,128)(2,1)} %param.21), kind=kOutput, calls=%fused_computation.47 | convolution fusion | flops 4307547136 | bytes 23093248 | tf_op jit(solution)/shard_map/dot_general | solution.py:187
  292.5 13.4 %multiply_reduce_fusion.4 = (f32[2048]{0:T(1024)}, bf16[1024,2048]{0,1:T(8,128)(2,1)}, bf16[1024,2048]{0,1:T(8,128)(2,1)}) fusion(bf16[1024,2304]{0,1:T(8,128)(2,1)} %copy-done.8, bf16[1024,2048]{0,1:T(8,128)(2,1)S(1)} %copy-done.36, f32[1024,2048]{0,1:T(8,128)S(1)} %copy-done.29, f32[1024]{0:T(1024)S(1)} %multiply_multiply_fusion.1, f32[1024]{0:T(1024)S(1)} %fusion.121, ...), kind=kLoop, calls=%fused_computation.51 | loop fusion | flops 50329600 | bytes 41967616 | tf_op jit(solution)/shard_map/transpose(jvp())/reduce_sum | solution.py:122
  313.4 11.2 %multiply_reduce_fusion.5 = (f32[8,2048]{1,0:T(8,128)}, bf16[128,2048]{1,0:T(8,128)(2,1)}, bf16[8,128,2048]{2,1,0:T(8,128)(2,1)}) fusion(f32[128,2048]{1,0:T(8,128)S(1)} %copy.257, f32[8,2048]{1,0:T(8,128)} %copy-done.38, f32[8,128,2048]{2,1,0:T(8,128)} %bitcast.364, f32[8,128,2048]{2,1,0:T(8,128)} %copy.266, bf16[16,8,8,128]{3,2,1,0:T(8,128)(2,1)} %get-tuple-element.105), kind=kOutput, calls=%fused_computation.52 | convolution fusion | flops 551272448 | bytes 22937600 | tf_op jit(solution)/shard_map/transpose(jvp(btn,bnc->btc))/dot_general | solution.py:115
  326.7 8.9 %convolution_convert_fusion.4 = bf16[1024,2048]{1,0:T(8,128)(2,1)} fusion(bf16[1024,2048]{0,1:T(8,128)(2,1)} %get-tuple-element.85, bf16[1024,1024]{1,0:T(8,128)(2,1)S(1)} %copy-done.27, f32[1024]{0:T(1024)S(1)} %copy-done.121, f32[1024]{0:T(1024)S(1)} %fusion.120), kind=kOutput, calls=%fused_computation.105 | convolution fusion | flops 4301258752 | bytes 10493952 | tf_op jit(solution)/shard_map/dot_general | solution.py:195
  347.5 9.8 %fusion.49 = bf16[8,128,128]{2,1,0:T(8,128)(2,1)S(1)} fusion(f32[8,128,2048]{2,1,0:T(8,128)} %bitcast.365, f32[8,128,2048]{2,1,0:T(8,128)} %copy.266, f32[8,128,2048]{2,1,0:T(8,128)} %add_dynamic-update-slice_fusion, f32[128,2048]{1,0:T(8,128)S(1)} %copy.257, f32[8,2048]{1,0:T(8,128)S(1)} %copy-done.39), kind=kOutput, calls=%fused_computation.119 | convolution fusion | flops 545390592 | bytes 26542080 | tf_op jit(solution)/shard_map/transpose(jvp(btn,bnc->btc))/dot_general | solution.py:115
  357.4 20.5 %fusion.10 = (f32[8,32,128]{2,1,0:T(8,128)}, f32[8,32,128]{2,1,0:T(8,128)}, f32[8,32,128]{2,1,0:T(8,128)}, bf16[8,128,128]{2,1,0:T(8,128)(2,1)S(1)}) fusion(f32[8,32,128]{2,1,0:T(8,128)S(1)} %copy-done.58, f32[8,32,128]{2,1,0:T(8,128)S(1)} %fusion.99, f32[8,128,128]{2,1,0:T(8,128)S(1)} %copy-done.49, pred[128,128]{1,0:T(8,128)(4,1)S(1)} %copy-done.86, ...), kind=kOutput, calls=%fused_computation.15 | convolution fusion | flops 607944704 | bytes 14041088 | tf_op jit(solution)/shard_map/transpose(jvp(bhts,bshp->bthp))/dot_general | solution.py:100
  386.9 10.0 %convolution_convert_fusion.5 = bf16[2048,1024]{1,0:T(8,128)(2,1)} fusion(bf16[1024,1024]{1,0:T(8,128)(2,1)S(1)} %copy-done.37, f32[1024,2048]{0,1:T(8,128)} %get-tuple-element.71, f32[2048]{0:T(1024)S(1)} %copy-done.115, f32[1024]{0:T(1024)S(1)} %copy-done.89), kind=kOutput, calls=%fused_computation.106 | convolution fusion | flops 4303355904 | bytes 14692352 | tf_op jit(solution)/shard_map/dot_general | solution.py:192
  452.0 9.3 %copy.272 = f32[8,128,2048]{1,2,0:T(8,128)} copy(f32[8,128,2048]{2,1,0:T(8,128)} %convert_convert_fusion) | data formatting | bytes 16777216 | tf_op jit(solution)/shard_map/transpose(jvp())/convert_element_type | solution.py:106
  461.3 15.3 %multiply_reduce_fusion.6 = (f32[8,128,32]{1,2,0:T(8,128)}, f32[8,128,32]{1,2,0:T(8,128)S(1)}) fusion(f32[8,128,32,64]{1,0,3,2:T(8,128)} %bitcast.381, f32[8,128,2048]{1,2,0:T(8,128)} %copy-done.9, f32[8,128,2048]{1,2,0:T(8,128)} %copy.272, f32[8,128,32,64]{1,0,3,2:T(8,128)} %bitcast.379), kind=kLoop, calls=%fused_computation.53 | loop fusion | flops 8323072 | bytes 33816576 | tf_op jit(solution)/shard_map/transpose(jvp())/reduce_sum | solution.py:121
  476.6 12.6 %fusion.36 = f32[8,128,32,64]{1,3,2,0:T(8,128)} fusion(f32[8,128,32,64]{1,3,2,0:T(8,128)S(1)} %bitcast.385, f32[8,128,32,64]{1,0,3,2:T(8,128)} %bitcast.382, f32[32]{0:T(128)S(1)} %copy-done.135, f32[8,128,32]{1,2,0:T(8,128)S(1)} %copy-done.44, f32[8,32,128]{2,1,0:T(8,128)S(1)} %copy-done.59, f32[8,32,128]{2,1,0:T(8,128)S(1)} %fusion.99, ...), kind=kOutput, calls=%fused_computation.92 | convolution fusion | flops 578813952 | bytes 30294144 | tf_op jit(solution)/shard_map/transpose(jvp(bhts,bshp->bthp))/dot_general | solution.py:100
  489.2 11.2 %copy.274 = f32[8,128,32,64]{1,0,3,2:T(8,128)S(1)} copy(f32[8,128,32,64]{1,3,2,0:T(8,128)} %fusion.36) | data formatting | bytes 16777216 | tf_op jit(solution)/shard_map/convert_element_type | solution.py:204
  511.7 27.6 %multiply_reduce_fusion.3 = (f32[2304]{0:T(1024)S(1)}, f32[2304]{0:T(1024)S(1)}, f32[2304]{0:T(1024)S(1)}, f32[2304]{0:T(1024)S(1)}, f32[2304]{0:T(1024)S(1)}, /*index=5*/f32[1024,2304]{0,1:T(8,128)}) fusion(f32[1027,2304]{0,1:T(8,128)} %copy-done, f32[1024,2304]{0,1:T(8,128)} %get-tuple-element.84, f32[1024,256]{0,1:T(8,128)S(1)} %convert_add_fusion.1, ...), kind=kLoop, calls=%fused_computation.30 | loop fusion | flops 44815104 | bytes 66106368 | tf_op jit(solution)/shard_map/transpose(jvp())/reduce_sum | solution.py:42
  539.3 10.5 %broadcast_multiply_fusion = (f32[1024,2304]{0,1:T(8,128)S(1)}, f32[1024,2304]{0,1:T(8,128)S(1)}, f32[1024,2304]{0,1:T(8,128)}, f32[1024,2304]{0,1:T(8,128)}) fusion(f32[1024,2304]{0,1:T(8,128)} %get-tuple-element.58, f32[2304]{0:T(1024)S(1)} %copy-done.69, f32[2304]{0:T(1024)S(1)} %copy-done.65, f32[2304]{0:T(1024)S(1)} %copy-done.67, f32[2304]{0:T(1024)S(1)} %copy-done.71), kind=kLoop, calls=%fused_computation.80 | loop fusion | flops 9437184 | bytes 47222784 | tf_op jit(solution)/shard_map/transpose(jvp())/mul | solution.py:42
  561.8 19.6 %pad_add_fusion = f32[1027,2304]{0,1:T(8,128)} fusion(f32[1024,2304]{0,1:T(8,128)} %copy-done.5, f32[1024,2304]{0,1:T(8,128)} %get-tuple-element.88, f32[1024,2304]{0,1:T(8,128)} %get-tuple-element.89, f32[1024,2304]{0,1:T(8,128)} %copy-done.4), kind=kLoop, calls=%fused_computation.21 | loop fusion | flops 7098624 | bytes 47213568 | tf_op jit(solution)/shard_map/transpose(jvp())/add_any | solution.py:42
  610.3 10.7 %fusion.33 = bf16[1024,1024]{1,0:T(8,128)(2,1)} fusion(bf16[1024,1024]{1,0:T(8,128)(2,1)S(1)} %copy-done.28, bf16[2048,1024]{1,0:T(8,128)(2,1)} %all-gather.13.cloned.1.call-done, f32[1024,2048]{0,1:T(8,128)} %get-tuple-element.71, f32[2048]{0:T(1024)S(1)} %copy-done.116, f32[1024]{0:T(1024)S(1)} %copy-done.90), kind=kOutput, calls=%fused_computation.89 | convolution fusion | flops 4304404480 | bytes 16789504 | tf_op jit(solution)/shard_map/dot_general | solution.py:184
  621.0 45.9 %reduce-scatter.18.cloned.1.call-done = bf16[128,2336]{1,0:T(8,128)(2,1)} async-done(((bf16[1024,2336]{1,0:T(8,128)(2,1)}), bf16[128,2336]{1,0:T(8,128)(2,1)}) %reduce-scatter.18.cloned.1.call-update) | async-done | bytes 598032
  669.9 10.0 %fusion.143 = f32[1024,1024]{1,0:T(8,128)} fusion(bf16[1024,2048]{0,1:T(8,128)(2,1)} %get-tuple-element.85, bf16[1024,2048]{0,1:T(8,128)(2,1)} %all-gather.11.cloned.1.call-done), kind=kOutput, calls=%fused_computation.292 | convolution fusion | flops 4294967296 | bytes 12582912 | tf_op jit(solution)/shard_map/dot_general | solution.py:217
  680.0 11.5 %fusion.29 = (f32[1024]{0:T(1024)S(1)}, f32[1024]{0:T(1024)S(1)}, f32[1024,1024]{1,0:T(8,128)}) fusion(bf16[1024,1024]{1,0:T(8,128)(2,1)S(1)} %copy-done.28, f32[1024]{0:T(1024)S(1)} %copy-done.84, f32[1024]{0:T(1024)S(1)} %copy-done.122, f32[1024,1024]{1,0:T(8,128)} %fusion.143, bf16[1024,2336]{0,1:T(8,128)(2,1)} %all-gather.7.cloned.1.call-done, ...), kind=kOutput, calls=%fused_computation.85 | convolution fusion | flops 4916901888 | bytes 20070400 | tf_op jit(solution)/shard_map/dot_general | solution.py:219
  691.6 43.8 %psum.7 = f32[14688]{0:T(1024)S(1)} all-reduce(f32[14688]{0:T(1024)S(1)} %concatenate.24), channel_id=1, replica_groups=mesh['dp'=8,'seq'=4] {'dp','seq'}, use_global_device_ids=true, to_apply=%region_44.45 | all-reduce | flops 14688 | bytes 117504 | tf_op jit(solution)/shard_map/psum | solution.py:228
  (477 shorter events, 256.4 us)
Async XLA Ops:
  7.2 46.0 %all-gather.7.cloned.1.call-start = ((), (), s32[]{:S(2)}) async-start(), calls=%async_computation.5 | async-start | bytes 5382144 | tf_op jit(solution)/shard_map/all_gather | solution.py:145
  9.2 202.3 %all-gather.9.cloned.1.call-start = ((), (), s32[]{:S(2)}) async-start(), calls=%async_computation.6 | async-start | bytes 2621440 | tf_op jit(solution)/shard_map/jvp()/all_gather | solution.py:62
  12.1 79.2 %copy-start.64 = (f32[2304]{0:T(1024)}, f32[2304]{0:T(1024)S(1)}, u32[]{:S(2)}) copy-start(f32[2304]{0:T(1024)S(1)} %get-tuple-element.50) | copy-start | bytes 27652
  12.2 79.2 %copy-start.66 = (f32[2304]{0:T(1024)}, f32[2304]{0:T(1024)S(1)}, u32[]{:S(2)}) copy-start(f32[2304]{0:T(1024)S(1)} %get-tuple-element.51) | copy-start | bytes 27652
  12.2 79.2 %copy-start.68 = (f32[2304]{0:T(1024)}, f32[2304]{0:T(1024)S(1)}, u32[]{:S(2)}) copy-start(f32[2304]{0:T(1024)S(1)} %get-tuple-element.52) | copy-start | bytes 27652
  12.2 79.2 %copy-start.70 = (f32[2304]{0:T(1024)}, f32[2304]{0:T(1024)S(1)}, u32[]{:S(2)}) copy-start(f32[2304]{0:T(1024)S(1)} %get-tuple-element.53) | copy-start | bytes 27652
  12.8 48.5 %copy-start.137 = (f32[32]{0:T(128)}, f32[32]{0:T(128)S(1)}, u32[]{:S(2)}) copy-start(f32[32]{0:T(128)S(1)} %exponential_negate_fusion) | copy-start | bytes 388
  15.5 311.2 %copy-start.83 = (f32[1024]{0:T(1024)}, f32[1024]{0:T(1024)S(1)}, u32[]{:S(2)}) copy-start(f32[1024]{0:T(1024)S(1)} %fusion.120) | copy-start | bytes 12292
  16.6 44.8 %copy-start.105 = (f32[32]{0:T(128)S(1)}, f32[32]{0:T(128)}, u32[]{:S(2)}) copy-start(f32[32]{0:T(128)} %param.16) | copy-start | bytes 388
  63.5 100.9 %copy-start.80 = (f32[8,32]{1,0:T(8,128)}, f32[8,32]{1,0:T(8,128)S(1)}, u32[]{:S(2)}) copy-start(f32[8,32]{1,0:T(8,128)S(1)} %get-tuple-element.115) | copy-start | bytes 3076
  63.8 22.3 %collective-permute-start = (bf16[3,2304]{1,0:T(4,128)(2,1)S(1)}, bf16[3,2304]{1,0:T(4,128)(2,1)S(1)}, u32[]{:S(2)}, u32[]{:S(2)}) collective-permute-start(bf16[3,2304]{1,0:T(4,128)(2,1)S(1)} %copy.238), channel_id=1, source_target_pairs={{0,1},{1,2},{2,3},{4,5},{5,6},{6,7},{8,9},{9,10},{10,11},{12,13},{... | collective-permute-start | bytes 41480 | tf_op jit(solution)/shard_map/ppermute | solution.py:16
  72.9 126.1 %copy-start.55 = (f32[2048]{0:T(1024)}, f32[2048]{0:T(1024)S(1)}, u32[]{:S(2)}) copy-start(f32[2048]{0:T(1024)S(1)} %mul.968) | copy-start | bytes 24580
  155.6 95.4 %all-gather.11.cloned.1.call-start = ((), (), s32[]{:S(2)}) async-start(), calls=%async_computation.7 | async-start | bytes 4718592 | tf_op jit(solution)/shard_map/all_gather | solution.py:149
  156.4 121.2 %all-gather.13.cloned.1.call-start = ((), (), s32[]{:S(2)}) async-start(), calls=%async_computation.8 | async-start | bytes 4718592 | tf_op jit(solution)/shard_map/all_gather | solution.py:150
  160.5 49.6 %copy-start.76 = (f32[2048]{0:T(1024)}, f32[2048]{0:T(1024)S(1)}, u32[]{:S(2)}) copy-start(f32[2048]{0:T(1024)S(1)} %mul.1001) | copy-start | bytes 24580
  161.3 48.8 %copy-start.62 = (f32[2048]{0:T(1024)}, f32[2048]{0:T(1024)S(1)}, u32[]{:S(2)}) copy-start(f32[2048]{0:T(1024)S(1)} %mul.996) | copy-start | bytes 24580
  162.1 45.5 %copy-start.60 = (f32[2048]{0:T(1024)}, f32[2048]{0:T(1024)S(1)}, u32[]{:S(2)}) copy-start(f32[2048]{0:T(1024)S(1)} %mul.991) | copy-start | bytes 24580
  162.8 42.0 %copy-start.72 = (f32[2048]{0:T(1024)}, f32[2048]{0:T(1024)S(1)}, u32[]{:S(2)}) copy-start(f32[2048]{0:T(1024)S(1)} %mul.986) | copy-start | bytes 24580
  163.6 38.2 %copy-start.74 = (f32[2048]{0:T(1024)}, f32[2048]{0:T(1024)S(1)}, u32[]{:S(2)}) copy-start(f32[2048]{0:T(1024)S(1)} %mul.981) | copy-start | bytes 24580
  164.6 52.5 %copy-start.38 = (f32[8,2048]{1,0:T(8,128)}, f32[8,2048]{1,0:T(8,128)S(1)}, u32[]{:S(2)}) copy-start(f32[8,2048]{1,0:T(8,128)S(1)} %mul.1005) | copy-start | bytes 196612
  189.8 207.3 %all-gather.15.cloned.1.call-start = ((), (), s32[]{:S(2)}) async-start(), calls=%async_computation.9 | async-start | bytes 2621440 | tf_op jit(solution)/shard_map/transpose(jvp())/all_gather | solution.py:112
  263.8 28.7 %copy-start.88 = (f32[1024]{0:T(1024)}, f32[1024]{0:T(1024)S(1)}, u32[]{:S(2)}) copy-start(f32[1024]{0:T(1024)S(1)} %fusion.121) | copy-start | bytes 12292
  326.6 273.2 %reduce-scatter.16.cloned.1.call-start = ((), (), s32[]{:S(2)}) async-start(), calls=%async_computation.12 | async-start | bytes 4718592
  335.6 265.6 %reduce-scatter.12.cloned.1.call-start = ((), (), s32[]{:S(2)}) async-start(), calls=%async_computation.10 | async-start | bytes 4718592 | tf_op jit(solution)/shard_map/reduce_scatter | solution.py:198
  397.0 269.9 %reduce-scatter.18.cloned.1.call-start = ((), (), s32[]{:S(2)}) async-start(), calls=%async_computation.13 | async-start | bytes 5603328
  476.6 29.5 %copy-start.45 = (f32[8,128,32]{1,2,0:T(8,128)}, f32[8,128,32]{1,2,0:T(8,128)S(1)}, u32[]{:S(2)}) copy-start(f32[8,128,32]{1,2,0:T(8,128)S(1)} %get-tuple-element.133) | copy-start | bytes 393220
  511.7 27.6 %copy-start.65 = (f32[2304]{0:T(1024)S(1)}, f32[2304]{0:T(1024)}, u32[]{:S(2)}) copy-start(f32[2304]{0:T(1024)} %copy-done.64) | copy-start | bytes 27652
  511.7 27.6 %copy-start.67 = (f32[2304]{0:T(1024)S(1)}, f32[2304]{0:T(1024)}, u32[]{:S(2)}) copy-start(f32[2304]{0:T(1024)} %copy-done.66) | copy-start | bytes 27652
  559.0 23.7 %collective-permute-start.1 = (f32[3,2304]{1,0:T(4,128)S(1)}, f32[3,2304]{1,0:T(4,128)}, u32[]{:S(2)}, u32[]{:S(2)}) collective-permute-start(f32[3,2304]{1,0:T(4,128)S(1)} %copy.281), channel_id=1, source_target_pairs={{1,0},{2,1},{3,2},{5,4},{6,5},{7,6},{9,8},{10,9},{11,10},{13,12},{... | collective-permute-start | bytes 82952 | tf_op jit(solution)/shard_map/ppermute | solution.py:16
  608.7 134.4 %reduce-scatter.14.cloned.1.call-start = ((), (), s32[]{:S(2)}) async-start(), calls=%async_computation.11 | async-start | bytes 1310720 | tf_op jit(solution)/shard_map/reduce_scatter | solution.py:225
  609.8 136.1 %reduce-scatter.20.cloned.1.call-start = ((), (), s32[]{:S(2)}) async-start(), calls=%async_computation.14 | async-start | bytes 2805760
  680.0 58.5 %copy-start.79 = (f32[1024]{0:T(1024)S(1)}, f32[1024]{0:T(1024)}, u32[]{:S(2)}) copy-start(f32[1024]{0:T(1024)} %copy-done.78) | copy-start | bytes 12292
  (126 other events, 1206.3 us)
Sparse Core Ops, SparseCore 0:
  10.5 42.7 all-gather.6
  155.7 45.2 all-gather.8
  202.9 36.1 all-gather.10
  240.8 36.7 all-gather.12
  326.8 45.9 all-gather.14
  375.9 50.0 reduce-scatter.15
  429.7 51.3 reduce-scatter.11
  608.8 58.0 reduce-scatter.17
  669.9 27.1 reduce-scatter.13
  699.8 46.0 reduce-scatter.19

commit v2 on v1

v2 whole, which is shorter than its diff:
```python
import jax
import jax.numpy as jnp
from jax import lax
from jax.experimental import pallas as pl
from jax.experimental.pallas import tpu as pltpu
from jax.sharding import PartitionSpec as P

BLOCK = 128


epsilon = 1e-05
highest = lax.Precision.HIGHEST


def passed_along(block, axis, distance):
    devices = range(lax.axis_size(axis))
    route = [(i - distance, i) for i in devices if i - distance in devices]
    return lax.ppermute(block, axis, route)


def front(inputs, gain_vector):
    return (
        inputs
        * lax.rsqrt(jnp.mean(inputs * inputs, axis=-1, keepdims=True) + epsilon)
        * gain_vector
    )


def gated_norm(mixed_values, gate_raw, gain_vector):
    gated_values = mixed_values * jax.nn.silu(gate_raw)
    return (
        gated_values
        * lax.rsqrt(jnp.mean(gated_values * gated_values, axis=-1, keepdims=True) + epsilon)
        * gain_vector
    )


def convolve(extended, kernel, offset_bias):
    tap_count = kernel.shape[0]
    rows_out = extended.shape[0] - tap_count + 1
    summed = jnp.broadcast_to(offset_bias[None, :], (rows_out, extended.shape[1]))
    for shift_index in range(tap_count):
        summed = (
            summed + kernel[shift_index][None, :] * extended[shift_index : shift_index + rows_out]
        )
    return jax.nn.silu(summed)


LANES = 128
low = jnp.bfloat16
wide = jnp.float32


def dot_nn(a, b):
    return lax.dot_general(a, b, (((1,), (0,)), ((), ())), preferred_element_type=wide)


def dot_nt(a, b):
    return lax.dot_general(a, b, (((1,), (1,)), ((), ())), preferred_element_type=wide)


def dot_tn(a, b):
    return lax.dot_general(a, b, (((0,), (0,)), ((), ())), preferred_element_type=wide)


def pair_columns(values, pair):
    rows = values.shape[0]
    left = lax.broadcasted_iota(jnp.int32, (rows, LANES), 1) < LANES // 2
    return jnp.where(
        left, values[:, 2 * pair : 2 * pair + 1], values[:, 2 * pair + 1 : 2 * pair + 2]
    )


def weighted_kernel(rows_ref, cols_ref, weight_ref, out_ref):
    @pl.when(pl.program_id(0) == 0)
    def _():
        out_ref[...] = jnp.zeros_like(out_ref)

    rows, weights = rows_ref[...], weight_ref[...]
    for pair in range(weights.shape[1] // 2):
        lanes = slice(pair * LANES, (pair + 1) * LANES)
        scaled = (cols_ref[:, lanes].astype(wide) * pair_columns(weights, pair)).astype(low)
        out_ref[:, lanes] += dot_tn(rows, scaled)


def block_decays(cum, cum_t, head, causal):
    gap = cum[:, head : head + 1] - cum_t[head : head + 1, :]
    return jnp.exp(jnp.where(causal, gap, -1e30))


def forward_kernel(
    x_ref, b_ref, c_ref, cum_ref, cum_t_ref, dt_ref, dt_t_ref, skip_ref, enter_ref,
    y_ref, kept_ref, state_ref,
):
    @pl.when(pl.program_id(0) == 0)
    def _():
        state_ref[...] = enter_ref[...]

    block_b, block_c = b_ref[...], c_ref[...]
    cum, cum_t, dt, dt_t = cum_ref[...], cum_t_ref[...], dt_ref[...], dt_t_ref[...]
    scores = dot_nt(block_c, block_b)
    row = lax.broadcasted_iota(jnp.int32, (BLOCK, BLOCK), 0)
    col = lax.broadcasted_iota(jnp.int32, (BLOCK, BLOCK), 1)
    causal = row >= col
    left = lax.broadcasted_iota(jnp.int32, (BLOCK, LANES), 1) < LANES // 2
    for pair in range(dt.shape[1] // 2):
        lanes = slice(pair * LANES, (pair + 1) * LANES)
        x = x_ref[:, lanes]
        x_wide = x.astype(wide)
        state = state_ref[:, lanes]
        state_low = state.astype(low)
        kept_ref[0, :, lanes] = state_low
        cums = pair_columns(cum, pair)
        final = cums[BLOCK - 1 :, :]
        inside = []
        for head in (2 * pair, 2 * pair + 1):
            mixing = scores * block_decays(cum, cum_t, head, causal) * dt_t[head : head + 1, :]
            inside.append(dot_nn(mixing.astype(low), x))
        y = (
            jnp.where(left, inside[0], inside[1])
            + jnp.exp(cums) * dot_nn(block_c, state_low)
            + skip_ref[:, lanes] * x_wide
        )
        y_ref[:, lanes] = y.astype(low)
        weighted = (x_wide * (jnp.exp(final - cums) * pair_columns(dt, pair))).astype(low)
        state_ref[:, lanes] = state * jnp.exp(final) + dot_tn(block_b, weighted)


def backward_kernel(
    x_ref, dy_ref, b_ref, c_ref, cum_ref, cum_t_ref, dt_ref, dt_t_ref, skip_ref, kept_ref,
    leave_ref,
    dx_ref, db_ref, dc_ref, row_ref, weight_ref, col_ref, state_sum_ref, skip_sum_ref, grad_ref,
):
    @pl.when(pl.program_id(0) == 0)
    def _():
        grad_ref[...] = leave_ref[...]

    block_b, block_c = b_ref[...], c_ref[...]
    cum, cum_t, dt, dt_t = cum_ref[...], cum_t_ref[...], dt_ref[...], dt_t_ref[...]
    heads = dt.shape[1]
    scores = dot_nt(block_c, block_b)
    row = lax.broadcasted_iota(jnp.int32, (BLOCK, BLOCK), 0)
    col = lax.broadcasted_iota(jnp.int32, (BLOCK, BLOCK), 1)
    causal = row >= col
    left = lax.broadcasted_iota(jnp.int32, (BLOCK, LANES), 1) < LANES // 2
    slot = lax.broadcasted_iota(jnp.int32, (BLOCK, heads), 1)
    row_sums = jnp.zeros((BLOCK, heads), wide)
    weight_sums = jnp.zeros((BLOCK, heads), wide)
    grad_scores = jnp.zeros((BLOCK, BLOCK), wide)
    grad_b = jnp.zeros((BLOCK, block_b.shape[1]), wide)
    grad_c = jnp.zeros((BLOCK, block_b.shape[1]), wide)
    for pair in range(heads // 2):
        lanes = slice(pair * LANES, (pair + 1) * LANES)
        x, dy = x_ref[:, lanes], dy_ref[:, lanes]
        x_wide, dy_wide = x.astype(wide), dy.astype(wide)
        state_low = kept_ref[0, :, lanes]
        grad = grad_ref[:, lanes]
        grad_low = grad.astype(low)
        cums = pair_columns(cum, pair)
        final = cums[BLOCK - 1 :, :]
        weights = jnp.exp(final - cums) * pair_columns(dt, pair)
        reached = dy_wide * jnp.exp(cums)
        reached_low = reached.astype(low)
        from_state = reached * dot_nn(block_c, state_low)
        to_state = dot_nn(block_b, grad_low)
        weighed = x_wide * to_state
        inside = []
        for side, head in enumerate((2 * pair, 2 * pair + 1)):
            mine = left if side == 0 else jnp.logical_not(left)
            decays = block_decays(cum, cum_t, head, causal)
            steps = dt_t[head : head + 1, :]
            plain = scores * decays
            mixing = (plain * steps).astype(low)
            inside.append(dot_tn(mixing, dy))
            grad_mixing = dot_nt(jnp.where(mine, dy, jnp.zeros_like(dy)), x)
            grad_plain = grad_mixing * plain
            grad_scores = grad_scores + grad_mixing * decays * steps
            sums = grad_plain * steps + jnp.where(mine, from_state, 0.0)
            row_sums = jnp.where(slot == head, jnp.sum(sums, axis=1, keepdims=True), row_sums)
            weight_sums = jnp.where(
                slot == head,
                jnp.sum(jnp.where(mine, weighed, 0.0), axis=1, keepdims=True),
                weight_sums,
            )
            col_ref[head : head + 1, :] = jnp.sum(grad_plain, axis=0, keepdims=True)
        dx_ref[:, lanes] = (
            jnp.where(left, inside[0], inside[1])
            + weights * to_state
            + skip_ref[:, lanes] * dy_wide
        ).astype(low)
        grad_c = grad_c + dot_nt(reached_low, state_low)
        grad_b = grad_b + dot_nt((x_wide * weights).astype(low), grad_low)
        state_sum_ref[0, :, lanes] = jnp.sum(
            grad * state_low.astype(wide), axis=0, keepdims=True
        )
        skip_sum_ref[0, :, lanes] = jnp.sum(dy_wide * x_wide, axis=0, keepdims=True)
        grad_ref[:, lanes] = grad * jnp.exp(final) + dot_tn(block_c, reached_low)
    scores_low = grad_scores.astype(low)
    dc_ref[...] = grad_c + dot_nn(scores_low, block_b)
    db_ref[...] = grad_b + dot_tn(scores_low, block_c)
    row_ref[...] = row_sums
    weight_ref[...] = weight_sums


def sequential():
    return pltpu.CompilerParams(
        dimension_semantics=("arbitrary",), vmem_limit_bytes=40 * 1024 * 1024
    )


def weighted_total(rows, cols, weights):
    length, states = rows.shape
    inner, heads = cols.shape[1], weights.shape[1]
    return pl.pallas_call(
        weighted_kernel,
        grid=(length // BLOCK,),
        in_specs=[
            pl.BlockSpec((BLOCK, states), lambda i: (i, 0)),
            pl.BlockSpec((BLOCK, inner), lambda i: (i, 0)),
            pl.BlockSpec((BLOCK, heads), lambda i: (i, 0)),
        ],
        out_specs=pl.BlockSpec((states, inner), lambda i: (0, 0)),
        out_shape=jax.ShapeDtypeStruct((states, inner), wide),
        compiler_params=sequential(),
        cost_estimate=pl.CostEstimate(
            flops=2 * length * states * inner, bytes_accessed=6 * length * inner, transcendentals=0
        ),
    )(rows, cols, weights)


def scan_specs(states, inner, heads, place):
    return dict(
        wide_rows=pl.BlockSpec((BLOCK, inner), lambda i: (place(i), 0)),
        state_rows=pl.BlockSpec((BLOCK, states), lambda i: (place(i), 0)),
        head_rows=pl.BlockSpec((BLOCK, heads), lambda i: (place(i), 0)),
        head_cols=pl.BlockSpec((heads, BLOCK), lambda i: (0, place(i))),
        skip=pl.BlockSpec((1, inner), lambda i: (0, 0)),
        state=pl.BlockSpec((states, inner), lambda i: (0, 0)),
        kept=pl.BlockSpec((1, states, inner), lambda i: (place(i), 0, 0)),
        sums=pl.BlockSpec((1, 1, inner), lambda i: (place(i), 0, 0)),
    )


def scan_forward(x, b, c, cum, cum_t, dt, dt_t, skip, enter):
    length, inner = x.shape
    states, heads = b.shape[1], dt.shape[1]
    blocks = length // BLOCK
    p = scan_specs(states, inner, heads, lambda i: i)
    return pl.pallas_call(
        forward_kernel,
        grid=(blocks,),
        in_specs=[
            p["wide_rows"], p["state_rows"], p["state_rows"], p["head_rows"], p["head_cols"],
            p["head_rows"], p["head_cols"], p["skip"], p["state"],
        ],
        out_specs=[p["wide_rows"], p["kept"]],
        out_shape=[
            jax.ShapeDtypeStruct((length, inner), low),
            jax.ShapeDtypeStruct((blocks, states, inner), low),
        ],
        scratch_shapes=[pltpu.VMEM((states, inner), wide)],
        compiler_params=sequential(),
        cost_estimate=pl.CostEstimate(
            flops=10 * length * states * inner, bytes_accessed=8 * length * inner,
            transcendentals=length * BLOCK * heads,
        ),
    )(x, b, c, cum, cum_t, dt, dt_t, skip, enter)


def scan_backward(x, dy, b, c, cum, cum_t, dt, dt_t, skip, kept, leave):
    length, inner = x.shape
    states, heads = b.shape[1], dt.shape[1]
    blocks = length // BLOCK
    p = scan_specs(states, inner, heads, lambda i: blocks - 1 - i)
    return pl.pallas_call(
        backward_kernel,
        grid=(blocks,),
        in_specs=[
            p["wide_rows"], p["wide_rows"], p["state_rows"], p["state_rows"], p["head_rows"],
            p["head_cols"], p["head_rows"], p["head_cols"], p["skip"], p["kept"], p["state"],
        ],
        out_specs=[
            p["wide_rows"], p["state_rows"], p["state_rows"], p["head_rows"], p["head_rows"],
            p["head_cols"], p["sums"], p["sums"],
        ],
        out_shape=[
            jax.ShapeDtypeStruct((length, inner), low),
            jax.ShapeDtypeStruct((length, states), wide),
            jax.ShapeDtypeStruct((length, states), wide),
            jax.ShapeDtypeStruct((length, heads), wide),
            jax.ShapeDtypeStruct((length, heads), wide),
            jax.ShapeDtypeStruct((heads, length), wide),
            jax.ShapeDtypeStruct((blocks, 1, inner), wide),
            jax.ShapeDtypeStruct((blocks, 1, inner), wide),
        ],
        scratch_shapes=[pltpu.VMEM((states, inner), wide)],
        compiler_params=sequential(),
        cost_estimate=pl.CostEstimate(
            flops=24 * length * states * inner, bytes_accessed=12 * length * inner,
            transcendentals=length * BLOCK * heads,
        ),
    )(x, dy, b, c, cum, cum_t, dt, dt_t, skip, kept, leave)


def state_space(x, dt_raw, b, c, dt_offset, log_rates, skip_gain):
    length, inner = x.shape
    heads, states = dt_raw.shape[1], b.shape[1]
    head_width = inner // heads
    blocks = length // BLOCK
    shifted = dt_raw.astype(wide) + dt_offset[None, :]
    dt = jax.nn.softplus(shifted)
    rate = -jnp.exp(log_rates)
    lower = (jnp.arange(BLOCK)[:, None] >= jnp.arange(BLOCK)[None, :]).astype(wide)
    cum_blocks = jnp.einsum(
        "ts,bsh->bth", lower, (dt * rate).reshape(blocks, BLOCK, heads), precision=highest
    )
    cum = cum_blocks.reshape(length, heads)
    final = cum_blocks[:, -1]
    reach = jnp.cumsum(final, axis=0)
    since = (cum_blocks + (reach - final)[:, None]).reshape(length, heads)
    total = reach[-1]
    added = weighted_total(b, x, jnp.exp(total[None] - since) * dt)
    decay = jnp.repeat(jnp.exp(total), head_width)[None]
    coarse = decay.astype(low)
    fine = (decay - coarse.astype(wide)).astype(low)
    sent = jnp.concatenate(
        [added.astype(low), coarse, fine, jnp.zeros((14, inner), low)], axis=0
    )
    everyone = lax.all_gather(sent, "seq")
    here, count = lax.axis_index("seq"), lax.axis_size("seq")
    decays = everyone[:, states].astype(wide) + everyone[:, states + 1].astype(wide)
    enter = jnp.zeros((states, inner), wide)
    for index in range(count - 1):
        moved = enter * decays[index][None] + everyone[index, :states].astype(wide)
        enter = jnp.where(index < here, moved, enter)
    cum_t, dt_t = cum.T, dt.T
    skip = jnp.repeat(skip_gain, head_width)[None]
    y, kept = scan_forward(x, b, c, cum, cum_t, dt, dt_t, skip, enter)

    def pull(dy):
        leaving = lax.all_gather(weighted_total(c, dy, jnp.exp(since)).astype(low), "seq")
        leave = jnp.zeros((states, inner), wide)
        for index in range(count - 1, 0, -1):
            moved = leave * decays[index][None] + leaving[index].astype(wide)
            leave = jnp.where(index > here, moved, leave)
        dx, db, dc, row_sums, weight_sums, col_sums, state_sums, skip_sums = scan_backward(
            x, dy, b, c, cum, cum_t, dt, dt_t, skip, kept, leave
        )
        columns = col_sums.T
        ended = jnp.exp(final[:, None] - cum_blocks).reshape(length, heads)
        through = weight_sums * ended * dt
        grad_cum = (row_sums - dt * columns - through).reshape(blocks, BLOCK, heads)
        kept_sums = jnp.sum(state_sums.reshape(blocks, heads, head_width), axis=2)
        grad_final = (
            jnp.sum(through.reshape(blocks, BLOCK, heads), axis=1) + jnp.exp(final) * kept_sums
        )
        grad_step = (
            jnp.einsum("ts,bth->bsh", lower, grad_cum, precision=highest) + grad_final[:, None]
        ).reshape(length, heads)
        grad_dt = columns + weight_sums * ended + grad_step * rate
        grad_raw = grad_dt * jax.nn.sigmoid(shifted)
        grad_skip = jnp.sum(skip_sums.reshape(blocks, heads, head_width), axis=(0, 2))
        return (
            dx, grad_raw, db, dc, jnp.sum(grad_raw, axis=0),
            rate * jnp.sum(grad_step * dt, axis=0), grad_skip,
        )

    return y, pull


def per_device(
    tokens,
    norm_gain,
    in_proj,
    conv_weight,
    conv_bias,
    dt_bias,
    a_log,
    skip_d,
    gate_norm,
    out_proj,
    cotangent,
):
    inner_width = gate_norm.shape[0]
    channels = conv_bias.shape[0]
    tap_count = conv_weight.shape[0]
    contract_rows = (((0,), (0,)), ((), ()))
    contract_cols = (((1,), (1,)), ((), ()))
    in_rest = lax.all_gather(in_proj[:, inner_width:], "dp", axis=0, tiled=True)
    gate_rows, out_rows, in_rest = lax.optimization_barrier(
        (in_proj[:, :inner_width], out_proj, in_rest)
    )
    in_gate = lax.all_gather(gate_rows, "dp", axis=0, tiled=True)
    out_full = lax.all_gather(out_rows, "dp", axis=0, tiled=True)
    inputs = tokens.astype(jnp.float32)
    normed, front_back = jax.vjp(front, inputs, norm_gain)
    normed_low = normed.astype(jnp.bfloat16)
    projected = jnp.dot(normed_low, in_rest, preferred_element_type=jnp.float32).astype(
        jnp.bfloat16
    )
    conv_in = projected[:, :channels]
    dt_raw = projected[:, channels:]
    rows_here = conv_in.shape[0]
    edge_rows = passed_along(conv_in[rows_here - (tap_count - 1) :], "seq", 1)
    extended = jnp.concatenate([edge_rows, conv_in], axis=0).astype(jnp.float32)
    activated, conv_back = jax.vjp(convolve, extended, conv_weight, conv_bias)
    states = (channels - inner_width) // 2
    activated = activated.astype(low)
    mixed, mixer_back = state_space(
        activated[:, :inner_width],
        dt_raw,
        activated[:, inner_width : inner_width + states],
        activated[:, inner_width + states :],
        dt_bias,
        a_log,
        skip_d,
    )
    gate_raw = jnp.dot(normed_low, in_gate, preferred_element_type=jnp.float32).astype(
        jnp.bfloat16
    )
    branch_in, tail_back = jax.vjp(
        gated_norm,
        mixed.astype(jnp.float32),
        gate_raw.astype(jnp.float32),
        gate_norm,
    )
    branch_low = branch_in.astype(jnp.bfloat16)
    block_out = (inputs + jnp.dot(branch_low, out_full, preferred_element_type=jnp.float32)).astype(
        jnp.bfloat16
    )
    grad_branch = lax.dot_general(
        cotangent, out_full, contract_cols, preferred_element_type=jnp.float32
    )
    grad_mixed, grad_gate_raw, grad_gate_norm = tail_back(grad_branch)
    grad_gate = grad_gate_raw.astype(jnp.bfloat16)
    grad_out_w = lax.dot_general(
        branch_low, cotangent, contract_rows, preferred_element_type=jnp.float32
    ).astype(jnp.bfloat16)
    grad_gate_w = lax.dot_general(
        normed_low, grad_gate, contract_rows, preferred_element_type=jnp.float32
    ).astype(jnp.bfloat16)
    part_out = lax.psum_scatter(grad_out_w, "dp", scatter_dimension=0, tiled=True)
    part_gate = lax.psum_scatter(grad_gate_w, "dp", scatter_dimension=0, tiled=True)
    grad_x, grad_dt, grad_b, grad_c, grad_offset, grad_alog, grad_skip = mixer_back(
        grad_mixed.astype(low)
    )
    grad_act = jnp.concatenate([grad_x.astype(wide), grad_b, grad_c], axis=1)
    grad_ext, grad_kernel, grad_cbias = conv_back(grad_act)
    edge_grad = passed_along(grad_ext[: tap_count - 1], "seq", -1)
    grad_conv_in = grad_ext[tap_count - 1 :] + jnp.concatenate(
        [jnp.zeros((rows_here - (tap_count - 1), channels), jnp.float32), edge_grad], axis=0
    )
    grad_rest = jnp.concatenate([grad_conv_in, grad_dt], axis=1).astype(jnp.bfloat16)
    grad_rest_w = lax.dot_general(
        normed_low, grad_rest, contract_rows, preferred_element_type=jnp.float32
    ).astype(jnp.bfloat16)
    grad_rest_w, part_out, part_gate = lax.optimization_barrier((grad_rest_w, part_out, part_gate))
    part_rest = lax.psum_scatter(grad_rest_w, "dp", scatter_dimension=0, tiled=True)
    grad_normed = lax.dot_general(
        grad_gate, in_gate, contract_cols, preferred_element_type=jnp.float32
    ) + lax.dot_general(grad_rest, in_rest, contract_cols, preferred_element_type=jnp.float32)
    grad_inputs, grad_gain = front_back(grad_normed)
    input_grad = (cotangent.astype(jnp.float32) + grad_inputs).astype(jnp.bfloat16)
    part_in = jnp.concatenate([part_gate, part_rest], axis=1).astype(jnp.float32)
    in_proj_grad, out_proj_grad = (
        lax.psum_scatter(part_in, "seq", scatter_dimension=1, tiled=True),
        lax.psum_scatter(part_out.astype(jnp.float32), "seq", scatter_dimension=1, tiled=True),
    )
    smalls = (grad_gain, grad_kernel, grad_cbias, grad_offset, grad_alog, grad_skip, grad_gate_norm)
    joined = jnp.concatenate([v.reshape(-1) for v in smalls])
    joined = jnp.pad(joined, (0, -joined.size % (8 * LANES))).reshape(-1, LANES)
    rows_sent = joined.shape[0]
    joined = lax.all_gather(joined, ("dp", "seq"), axis=0, tiled=True)
    joined = jnp.sum(joined.reshape(-1, rows_sent, LANES), axis=0).reshape(-1)
    small_sums, start = [], 0
    for value in smalls:
        small_sums.append(joined[start : start + value.size].reshape(value.shape))
        start += value.size
    return (
        block_out,
        input_grad,
        small_sums[0],
        in_proj_grad,
        *small_sums[1:],
        out_proj_grad,
    )


def solution(mesh):
    in_specs = (
        P(("dp", "seq"), None),
        P(),
        P("dp", None),
        P(),
        P(),
        P(),
        P(),
        P(),
        P(),
        P("dp", None),
        P(("dp", "seq"), None),
    )
    out_specs = (
        P(("dp", "seq"), None),
        P(("dp", "seq"), None),
        P(),
        P("dp", "seq"),
        P(),
        P(),
        P(),
        P(),
        P(),
        P(),
        P("dp", "seq"),
    )
    return jax.shard_map(
        per_device, mesh=mesh, in_specs=in_specs, out_specs=out_specs, check_vma=False
    )
```

time: 760 us -> 694 us (0.913)
  waiting for transfers between devices: 100 us -> 297 us
  local copies, waits for them, and re-layouts: 197 us -> 72.1 us
  Pallas kernels: 0 us -> 83 us
  other arithmetic: 202 us -> 119 us
  matrix products: 177 us -> 96.4 us
  blocking collectives: 53.9 us -> 0 us
    all_gather x2 -> x3, waiting for transfers between devices: 0.02 us -> 111 us  [the longest x1 47.1 us: state_space(): everyone = lax.all_gather(sent, 'seq')]
    pallas_call x0 -> x4, Pallas kernels: none -> 83 us  [the longest x1 52.8 us: scan_backward(): pl.pallas_call(backward_kernel, grid=(blocks,), in_specs=[p['wide_rows'],...]
    dot_general x14 -> x2, matrix products: 83.3 us -> 0.45 us  [the longest x1 0.24 us: state_space(): jnp.einsum('ts,bsh->bth', lower, (dt * rate).reshape(blocks, BLOCK, heads...]
    reduce_sum x16 -> x6, other arithmetic: 50.2 us -> 3.18 us  [the longest x1 1.65 us: per_device(): joined = jnp.sum(joined.reshape(-1, rows_sent, LANES), axis=0).reshape(-1)]
    psum x1 -> x0, blocking collectives: 43.8 us -> none  [per_device(): lax.psum(jnp.concatenate([v.reshape(-1) for v in smalls]), ('dp', 'seq'))]
    convert_element_type x5 -> x0, local copies, waits for them, and re-layouts: 41.1 us -> none  [the longest x1 11.2 us: per_device(): grad_x.astype(jnp.bfloat16).astype(jnp.float32)]
    mul x21 -> x1, local copies, waits for them, and re-layouts: 31.6 us -> 0.19 us  [state_space(): added = weighted_total(b, x, jnp.exp(total[None] - since) * dt)]
    unnamed x13 -> x14, waiting for transfers between devices: 49.5 us -> 80.2 us
  transfers between devices with their start and end apart: 12 -> 13, of which waited for: 4 -> 9; matrix products, arithmetic and copies ran while one was open for 56% -> 28% of each run, Pallas kernels for 0% -> 10%
where the time goes in v2:
time: 694 us; the launch traced here: 689 us
  waiting for transfers between devices  297 us (43%)
  other arithmetic  119 us (17%)
  matrix products  96.4 us (14%)
  Pallas kernels  83 us (12%)
  local copies, waits for them, and re-layouts  72.1 us (10%)
  between operations  15.1 us (2%)
    unnamed x14, waiting for transfers between devices  80.2 us
    pallas_call x1, Pallas kernels, scan_backward(): pl.pallas_call(backward_kernel, grid=(blocks,), in_specs=[p['wide_rows'],...  52.8 us
    all_gather x1, waiting for transfers between devices, state_space(): everyone = lax.all_gather(sent, 'seq')  47.1 us
    all_gather x1, waiting for transfers between devices, per_device(): joined = lax.all_gather(joined, ('dp', 'seq'), axis=0, tiled=True)  42.1 us
    all_gather x1, waiting for transfers between devices, per_device(): in_rest = lax.all_gather(in_proj[:, inner_width:], 'dp', axis=0, tiled=True)  37.5 us
    unnamed x103, local copies, waits for them, and re-layouts  34.7 us
    reduce_sum x1, other arithmetic, convolve(): kernel[shift_index][None, :] * extended[shift_index:shift_index + rows_out]  27.8 us
    all_gather x1, waiting for transfers between devices, per_device(): out_full = lax.all_gather(out_rows, 'dp', axis=0, tiled=True)  27.5 us
  transfers between devices with their start and end apart: 13, of which 9 were waited for; matrix products, arithmetic and copies ran while one was open for 28% of the time, Pallas kernels for 10%

profile of v2, /device:TPU:0, one launch (start us, length us, event | category | flops | bytes accessed | tf_op | source)
XLA Modules:
  0.0 688.7 jit_solution(905684876932197405)
XLA Ops:
  15.7 37.5 %all-gather.9.cloned.1.call-done = bf16[1024,2336]{0,1:T(8,128)(2,1)} async-done(((bf16[128,2336]{0,1:T(8,128)(2,1)}), bf16[1024,2336]{0,1:T(8,128)(2,1)}) %all-gather.9.cloned.1.call-update) | async-done | bytes 4784144 | tf_op jit(solution)/shard_map/all_gather | solution.py:389
  53.3 8.2 %convolution_convert_fusion.1 = bf16[1024,2336]{0,1:T(8,128)(2,1)S(1)} fusion(bf16[1024,2336]{0,1:T(8,128)(2,1)} %all-gather.9.cloned.1.call-done, bf16[1024,1024]{1,0:T(8,128)(2,1)S(1)} %copy-done.16, f32[1024]{0:T(1024)S(1)} %copy-done.43, f32[1024]{0:T(1024)S(1)} %fusion.48), kind=kOutput, calls=%fused_computation.41 | convolution fusion | flops 4905533440 | bytes 11673600 | tf_op jit(solution)/shard_map/dot_general | solution.py:398
  81.7 11.8 %multiply_convert_fusion = (bf16[1024,2304]{0,1:T(8,128)(2,1)S(1)}, f32[1024,2304]{0,1:T(8,128)}) fusion(f32[1027,2304]{0,1:T(8,128)S(1)} %maximum_convert_fusion, f32[2304]{0:T(1024)S(1)} %get-tuple-element.54, f32[2304]{0:T(1024)S(1)} %get-tuple-element.55, f32[2304]{0:T(1024)S(1)} %get-tuple-element.53, f32[2304]{0:T(1024)S(1)} %get-tuple-element.52, ...), kind=kLoop, calls=%fused_computation.18 | loop fusion | flops 30670848 | bytes 51950592 | tf_op jit(solution)/shard_map/convert_element_type | solution.py:408
  96.0 6.5 copy.162.cols_ref.x_ref
  104.8 7.3 %shard_map.194 = f32[128,2048]{1,0:T(8,128)S(1)} custom-call(bf16[1024,128]{1,0:T(8,128)(2,1)S(1)} %copy.163.rows_ref.b_ref, bf16[1024,2048]{1,0:T(8,128)(2,1)S(1)} %copy-done, f32[1024,32]{1,0:T(8,128)S(1)} %copy.161.weight_ref), custom_call_target="tpu_custom_call" | custom-call | flops 536870912 | bytes 12582912 | tf_op jit(solution)/shard_map/pallas_call | solution.py:214
  115.8 47.1 %all-gather.17.cloned.1.call-done = bf16[576,2048]{1,0:T(8,128)(2,1)} async-done(((bf16[144,2048]{1,0:T(8,128)(2,1)}), bf16[576,2048]{1,0:T(8,128)(2,1)}) %all-gather.17.cloned.1.call-update) | async-done | bytes 2359312 | tf_op jit(solution)/shard_map/all_gather | solution.py:329
  165.7 15.6 %shard_map.195 = (bf16[1024,2048]{1,0:T(8,128)(2,1)S(1)}, bf16[8,128,2048]{2,1,0:T(8,128)(2,1)S(1)}) custom-call(bf16[1024,2048]{1,0:T(8,128)(2,1)} %copy.162.cols_ref.x_ref, bf16[1024,128]{1,0:T(8,128)(2,1)S(1)} %copy.163.rows_ref.b_ref, bf16[1024,128]{1,0:T(8,128)(2,1)S(1)} %copy.164.c_ref.rows_ref, f32[1024,32]{1,0:T(8,128)S(1)} %copy.165.cum_ref, ...), custom_call_target="tpu_custom_call" | custom-call | flops 2684354560 | bytes 16777216 | tf_op jit(solution)/shard_map/pallas_call | solution.py:249
  185.4 16.3 %all-gather.11.cloned.1.call-done = bf16[1024,2048]{0,1:T(8,128)(2,1)} async-done(((bf16[128,2048]{0,1:T(8,128)(2,1)}), bf16[1024,2048]{0,1:T(8,128)(2,1)}) %all-gather.11.cloned.1.call-update) | async-done | bytes 4194320 | tf_op jit(solution)/shard_map/all_gather | solution.py:393
  201.7 11.0 %multiply_reduce_fusion.5 = (f32[1024]{0:T(1024)S(1)}, bf16[1024,2048]{1,0:T(8,128)(2,1)}) fusion(bf16[1024,2048]{1,0:T(8,128)(2,1)} %copy-done.4, bf16[1024,2048]{0,1:T(8,128)(2,1)} %all-gather.11.cloned.1.call-done, bf16[1024,1024]{1,0:T(8,128)(2,1)} %param.11, f32[1024]{0:T(1024)S(1)} %copy-done.43, f32[1024]{0:T(1024)S(1)} %fusion.48), kind=kOutput, calls=%fused_computation.33 | convolution fusion | flops 4320132096 | bytes 14692352 | tf_op jit(solution)/shard_map/dot_general | solution.py:418
  212.6 27.5 %all-gather.13.cloned.1.call-done = bf16[2048,1024]{1,0:T(8,128)(2,1)} async-done(((bf16[256,1024]{1,0:T(8,128)(2,1)}), bf16[2048,1024]{1,0:T(8,128)(2,1)}) %all-gather.13.cloned.1.call-update) | async-done | bytes 4194320 | tf_op jit(solution)/shard_map/all_gather | solution.py:394
  240.2 12.3 %fusion.9 = (f32[2048]{0:T(1024)}, f32[1024]{0:T(1024)S(1)}, f32[2048,1024]{0,1:T(8,128)S(1)}) fusion(f32[1024]{0:T(1024)S(1)} %fusion.49, bf16[1024,2048]{1,0:T(8,128)(2,1)} %get-tuple-element.90, bf16[1024,2048]{1,0:T(8,128)(2,1)} %copy-done.4, f32[2048]{0:T(1024)S(1)} %copy-done.37, bf16[2048,1024]{1,0:T(8,128)(2,1)} %all-gather.13.cloned.1.call-done, ...), kind=kOutput, calls=%fused_computation.29 | convolution fusion | flops 4322227200 | bytes 23093248 | tf_op jit(solution)/shard_map/dot_general | solution.py:431
  252.5 8.3 %multiply_convert_fusion.1 = (bf16[1024,2048]{1,0:T(8,128)(2,1)S(1)}, bf16[1024,2048]{1,0:T(8,128)(2,1)}) fusion(f32[1024]{0:T(1024)S(1)} %multiply_multiply_fusion.1, f32[2048,1024]{0,1:T(8,128)S(1)} %get-tuple-element.91, f32[2048]{0:T(1024)S(1)} %copy-done.37, f32[1024]{0:T(1024)S(1)} %fusion.49, bf16[1024,2048]{1,0:T(8,128)(2,1)S(1)} %copy-done.21, ...), kind=kLoop, calls=%fused_computation.30 | loop fusion | flops 46137344 | bytes 25182208 | tf_op jit(solution)/shard_map/convert_element_type | solution.py:445
  260.8 7.3 %shard_map.196 = f32[128,2048]{1,0:T(8,128)S(1)} custom-call(bf16[1024,128]{1,0:T(8,128)(2,1)S(1)} %copy.164.c_ref.rows_ref, bf16[1024,2048]{1,0:T(8,128)(2,1)S(1)} %get-tuple-element.61.cols_ref.dy_ref, f32[1024,32]{1,0:T(8,128)S(1)} %copy.169.weight_ref), custom_call_target="tpu_custom_call" | custom-call | flops 536870912 | bytes 12582912 | tf_op jit(solution)/shard_map/pallas_call | solution.py:214
  271.6 9.7 %convolution_convert_fusion.2 = bf16[1024,2048]{1,0:T(8,128)(2,1)} fusion(bf16[1024,2048]{1,0:T(8,128)(2,1)} %get-tuple-element.62, bf16[1024,1024]{1,0:T(8,128)(2,1)} %param.11, f32[1024]{0:T(1024)S(1)} %copy-done.43, f32[1024]{0:T(1024)S(1)} %fusion.48), kind=kOutput, calls=%fused_computation.57 | convolution fusion | flops 4301258752 | bytes 10493952 | tf_op jit(solution)/shard_map/dot_general | solution.py:439
  282.2 12.6 %convolution_convert_fusion.3 = bf16[2048,1024]{1,0:T(8,128)(2,1)} fusion(bf16[1024,1024]{1,0:T(8,128)(2,1)} %param.21, f32[2048]{0:T(1024)S(1)} %copy-done.37, f32[1024]{0:T(1024)S(1)} %fusion.49, bf16[1024,2048]{1,0:T(8,128)(2,1)} %copy-done.4, bf16[1024,2048]{1,0:T(8,128)(2,1)} %get-tuple-element.90), kind=kOutput, calls=%fused_computation.58 | convolution fusion | flops 4318035968 | bytes 14692352 | tf_op jit(solution)/shard_map/dot_general | solution.py:436
  295.0 22.1 %all-gather.19.cloned.1.call-done = bf16[512,2048]{1,0:T(8,128)(2,1)} async-done(((bf16[128,2048]{1,0:T(8,128)(2,1)}), bf16[512,2048]{1,0:T(8,128)(2,1)}) %all-gather.19.cloned.1.call-update) | async-done | bytes 2097168 | tf_op jit(solution)/shard_map/all_gather | solution.py:341
  321.1 52.8 %shard_map.197 = (bf16[1024,2048]{1,0:T(8,128)(2,1)S(1)}, f32[1024,128]{1,0:T(8,128)S(1)}, f32[1024,128]{1,0:T(8,128)S(1)}, f32[1024,32]{1,0:T(8,128)S(1)}, f32[...) custom-call(bf16[1024,2048]{1,0:T(8,128)(2,1)S(1)} %copy-done.1, ...), custom_call_target="tpu_custom_call" | custom-call | flops 6442450944 | bytes 25165824 | tf_op jit(solution)/shard_map/pallas_call | solution.py:275
  377.9 6.6 copy.175
  386.8 6.7 convert_element_type.187
  393.6 27.8 %multiply_reduce_fusion.3 = (f32[2304]{0:T(1024)S(1)}, f32[2304]{0:T(1024)S(1)}, f32[2304]{0:T(1024)S(1)}, f32[2304]{0:T(1024)S(1)}, f32[2304]{0:T(1024)S(1)}, /*index=5*/f32[1024,2304]{0,1:T(8,128)}) fusion(f32[1027,2304]{0,1:T(8,128)} %copy-done.13, f32[1024,2304]{0,1:T(8,128)} %get-tuple-element.60, f32[1024,128]{0,1:T(8,128)S(1)} %copy.177, ...), kind=kLoop, calls=%fused_computation.17 | loop fusion | flops 47174400 | bytes 66106368 | tf_op jit(solution)/shard_map/transpose(jvp())/reduce_sum | solution.py:44
  421.4 10.5 %broadcast_multiply_fusion = (f32[1024,2304]{0,1:T(8,128)S(1)}, f32[1024,2304]{0,1:T(8,128)S(1)}, f32[1024,2304]{0,1:T(8,128)}, f32[1024,2304]{0,1:T(8,128)}) fusion(f32[1024,2304]{0,1:T(8,128)} %get-tuple-element.58, f32[2304]{0:T(1024)S(1)} %copy-done.31, f32[2304]{0:T(1024)S(1)} %copy-done.27, f32[2304]{0:T(1024)S(1)} %copy-done.29, f32[2304]{0:T(1024)S(1)} %copy-done.33), kind=kLoop, calls=%fused_computation.46 | loop fusion | flops 9437184 | bytes 47222784 | tf_op jit(solution)/shard_map/transpose(jvp())/mul | solution.py:44
  443.3 19.7 %pad_add_fusion = f32[1027,2304]{0,1:T(8,128)} fusion(f32[1024,2304]{0,1:T(8,128)} %copy-done.15, f32[1024,2304]{0,1:T(8,128)} %get-tuple-element.65, f32[1024,2304]{0,1:T(8,128)} %get-tuple-element.66, f32[1024,2304]{0,1:T(8,128)} %copy-done.14), kind=kLoop, calls=%fused_computation.6 | loop fusion | flops 7098624 | bytes 47213568 | tf_op jit(solution)/shard_map/transpose(jvp())/add_any | solution.py:44
  464.6 6.3 fusion.2
  473.1 7.6 %convolution_convert_fusion = bf16[1024,2336]{0,1:T(8,128)(2,1)} fusion(bf16[1024,32]{0,1:T(8,128)(2,1)S(1)} %get-tuple-element.57, bf16[1024,2304]{0,1:T(8,128)(2,1)S(1)} %fusion.2, bf16[1024,1024]{1,0:T(8,128)(2,1)S(1)} %copy-done.17, f32[1024]{0:T(1024)S(1)} %copy-done.44, f32[1024]{0:T(1024)S(1)} %fusion.48), kind=kOutput, calls=%fused_computation.40 | convolution fusion | flops 4915101696 | bytes 11673600 | tf_op jit(solution)/shard_map/dot_general | solution.py:454
  482.1 7.4 %copy.194 = bf16[1024,2336]{1,0:T(8,128)(2,1)} copy(bf16[1024,2336]{0,1:T(8,128)(2,1)} %convolution_convert_fusion) | data formatting | bytes 9568256
  489.6 10.0 %fusion.66 = f32[1024,1024]{1,0:T(8,128)} fusion(bf16[1024,2048]{1,0:T(8,128)(2,1)} %get-tuple-element.62, bf16[1024,2048]{0,1:T(8,128)(2,1)} %all-gather.11.cloned.1.call-done), kind=kOutput, calls=%fused_computation.149 | convolution fusion | flops 4294967296 | bytes 12582912 | tf_op jit(solution)/shard_map/dot_general | solution.py:459
  500.0 12.8 %fusion.13 = (f32[1024]{0:T(1024)S(1)}, f32[1024]{0:T(1024)S(1)}, f32[1024,1024]{1,0:T(8,128)}) fusion(bf16[1024,1024]{1,0:T(8,128)(2,1)S(1)} %copy-done.17, f32[1024]{0:T(1024)S(1)} %fusion.48, f32[1024]{0:T(1024)S(1)} %copy-done.44, f32[1024,1024]{1,0:T(8,128)} %fusion.66, bf16[1024,2336]{0,1:T(8,128)(2,1)} %all-gather.9.cloned.1.call-done, ...), kind=kOutput, calls=%fused_computation.51 | convolution fusion | flops 4916901888 | bytes 20070400 | tf_op jit(solution)/shard_map/dot_general | solution.py:461
  514.7 30.8 %reduce-scatter.18.cloned.1.call-done = bf16[128,2336]{1,0:T(8,128)(2,1)} async-done(((bf16[1024,2336]{1,0:T(8,128)(2,1)}), bf16[128,2336]{1,0:T(8,128)(2,1)}) %reduce-scatter.18.cloned.1.call-update) | async-done | bytes 598032
  548.5 11.8 %fusion.17 = bf16[1024,1024]{1,0:T(8,128)(2,1)} fusion(bf16[1024,1024]{1,0:T(8,128)(2,1)S(1)} %copy-done.17, bf16[2048,1024]{1,0:T(8,128)(2,1)} %all-gather.13.cloned.1.call-done, f32[2048]{0:T(1024)S(1)} %copy-done.38, f32[1024]{0:T(1024)S(1)} %fusion.49, bf16[1024,2048]{1,0:T(8,128)(2,1)} %copy-done.4, bf16[1024,2048]{1,0:T(8,128)(2,1)} %get-tuple-element.90), kind=kOutput, calls=%fused_computation.55 | convolution fusion | flops 4319084544 | bytes 16789504 | tf_op jit(solution)/shard_map/dot_general | solution.py:428
  562.8 42.1 %all-gather.15.cloned.1.call-done = f32[3840,128]{1,0:T(8,128)} async-done(((f32[120,128]{1,0:T(8,128)}), f32[3840,128]{1,0:T(8,128)}) %all-gather.15.cloned.1.call-update) | async-done | bytes 1966096 | tf_op jit(solution)/shard_map/all_gather | solution.py:473
  609.7 24.1 %reduce-scatter.14.cloned.1.call-done = f32[256,256]{1,0:T(8,128)} async-done(((f32[256,1024]{1,0:T(8,128)}), f32[256,256]{1,0:T(8,128)}) %reduce-scatter.14.cloned.1.call-update) | async-done | bytes 262160 | tf_op jit(solution)/shard_map/reduce_scatter | solution.py:467
  633.7 48.0 %reduce-scatter.20.cloned.1.call-done = f32[128,1096]{0,1:T(8,128)} async-done(((f32[128,4384]{0,1:T(8,128)}), f32[128,1096]{0,1:T(8,128)}) %reduce-scatter.20.cloned.1.call-update) | async-done | bytes 561168
  (217 shorter events, 87.6 us)
Async XLA Ops:
  7.2 46.1 %copy-start.16 = (bf16[1024,1024]{1,0:T(8,128)(2,1)S(1)}, bf16[1024,1024]{1,0:T(8,128)(2,1)}, u32[]{:S(2)}) copy-start(bf16[1024,1024]{1,0:T(8,128)(2,1)} %param.11) | copy-start | bytes 6291460
  7.2 46.1 %copy-start.43 = (f32[1024]{0:T(1024)S(1)}, f32[1024]{0:T(1024)}, u32[]{:S(2)}) copy-start(f32[1024]{0:T(1024)} %param.12) | copy-start | bytes 12292
  7.2 46.0 %all-gather.9.cloned.1.call-start = ((), (), s32[]{:S(2)}) async-start(), calls=%async_computation.5 | async-start | bytes 5382144 | tf_op jit(solution)/shard_map/all_gather | solution.py:389
  9.3 153.6 %all-gather.17.cloned.1.call-start = ((), (), s32[]{:S(2)}) async-start(), calls=%async_computation.11 | async-start | bytes 2949120 | tf_op jit(solution)/shard_map/all_gather | solution.py:329
  12.4 69.3 %copy-start.26 = (f32[2304]{0:T(1024)}, f32[2304]{0:T(1024)S(1)}, u32[]{:S(2)}) copy-start(f32[2304]{0:T(1024)S(1)} %get-tuple-element.52) | copy-start | bytes 27652
  12.4 69.3 %copy-start.28 = (f32[2304]{0:T(1024)}, f32[2304]{0:T(1024)S(1)}, u32[]{:S(2)}) copy-start(f32[2304]{0:T(1024)S(1)} %get-tuple-element.53) | copy-start | bytes 27652
  12.4 69.3 %copy-start.30 = (f32[2304]{0:T(1024)}, f32[2304]{0:T(1024)S(1)}, u32[]{:S(2)}) copy-start(f32[2304]{0:T(1024)S(1)} %get-tuple-element.54) | copy-start | bytes 27652
  12.4 69.3 %copy-start.32 = (f32[2304]{0:T(1024)}, f32[2304]{0:T(1024)S(1)}, u32[]{:S(2)}) copy-start(f32[2304]{0:T(1024)S(1)} %get-tuple-element.55) | copy-start | bytes 27652
  13.1 48.4 %copy-start.45 = (f32[32]{0:T(128)}, f32[32]{0:T(128)S(1)}, u32[]{:S(2)}) copy-start(f32[32]{0:T(128)S(1)} %exponential_negate_fusion) | copy-start | bytes 388
  15.7 47.9 %copy-start.40 = (f32[32]{0:T(128)S(1)}, f32[32]{0:T(128)}, u32[]{:S(2)}) copy-start(f32[32]{0:T(128)} %param.16) | copy-start | bytes 388
  66.2 10.1 %collective-permute-start = (bf16[3,2304]{1,0:T(4,128)(2,1)S(1)}, bf16[3,2304]{1,0:T(4,128)(2,1)S(1)}, u32[]{:S(2)}, u32[]{:S(2)}) collective-permute-start(bf16[3,2304]{1,0:T(4,128)(2,1)S(1)} %copy.153), channel_id=1, source_target_pairs={{0,1},{1,2},{2,3},{4,5},{5,6},{6,7},{8,9},{9,10},{10,11},{12,13},{... | collective-permute-start | bytes 41480 | tf_op jit(solution)/shard_map/ppermute | solution.py:18
  113.2 88.5 %all-gather.11.cloned.1.call-start = ((), (), s32[]{:S(2)}) async-start(), calls=%async_computation.6 | async-start | bytes 4718592 | tf_op jit(solution)/shard_map/all_gather | solution.py:393
  113.9 126.2 %all-gather.13.cloned.1.call-start = ((), (), s32[]{:S(2)}) async-start(), calls=%async_computation.7 | async-start | bytes 4718592 | tf_op jit(solution)/shard_map/all_gather | solution.py:394
  114.5 202.6 %all-gather.19.cloned.1.call-start = ((), (), s32[]{:S(2)}) async-start(), calls=%async_computation.12 | async-start | bytes 2621440 | tf_op jit(solution)/shard_map/all_gather | solution.py:341
  201.7 38.5 %copy-start.37 = (f32[2048]{0:T(1024)S(1)}, f32[2048]{0:T(1024)}, u32[]{:S(2)}) copy-start(f32[2048]{0:T(1024)} %param.19) | copy-start | bytes 24580
  240.2 12.3 %copy-start.21 = (bf16[1024,2048]{1,0:T(8,128)(2,1)S(1)}, bf16[1024,2048]{1,0:T(8,128)(2,1)}, u32[]{:S(2)}) copy-start(bf16[1024,2048]{1,0:T(8,128)(2,1)} %get-tuple-element.90) | copy-start | bytes 12582916
  271.0 209.7 %reduce-scatter.16.cloned.1.call-start = ((), (), s32[]{:S(2)}) async-start(), calls=%async_computation.13 | async-start | bytes 4718592
  281.3 200.8 %reduce-scatter.12.cloned.1.call-start = ((), (), s32[]{:S(2)}) async-start(), calls=%async_computation.9 | async-start | bytes 4718592 | tf_op jit(solution)/shard_map/reduce_scatter | solution.py:442
  294.8 250.8 %reduce-scatter.18.cloned.1.call-start = ((), (), s32[]{:S(2)}) async-start(), calls=%async_computation.14 | async-start | bytes 5603328
  393.6 27.8 %copy-start.27 = (f32[2304]{0:T(1024)S(1)}, f32[2304]{0:T(1024)}, u32[]{:S(2)}) copy-start(f32[2304]{0:T(1024)} %copy-done.26) | copy-start | bytes 27652
  393.6 27.8 %copy-start.29 = (f32[2304]{0:T(1024)S(1)}, f32[2304]{0:T(1024)}, u32[]{:S(2)}) copy-start(f32[2304]{0:T(1024)} %copy-done.28) | copy-start | bytes 27652
  393.6 27.8 %copy-start.31 = (f32[2304]{0:T(1024)S(1)}, f32[2304]{0:T(1024)}, u32[]{:S(2)}) copy-start(f32[2304]{0:T(1024)} %copy-done.30) | copy-start | bytes 27652
  393.6 27.8 %copy-start.33 = (f32[2304]{0:T(1024)S(1)}, f32[2304]{0:T(1024)}, u32[]{:S(2)}) copy-start(f32[2304]{0:T(1024)} %copy-done.32) | copy-start | bytes 27652
  441.0 23.1 %collective-permute-start.1 = (f32[3,2304]{1,0:T(4,128)S(1)}, f32[3,2304]{1,0:T(4,128)S(1)}, u32[]{:S(2)}, u32[]{:S(2)}) collective-permute-start(f32[3,2304]{1,0:T(4,128)S(1)} %copy.178), channel_id=1, source_target_pairs={{1,0},{2,1},{3,2},{5,4},{6,5},{7,6},{9,8},{10,9},{11,10},{13,12},{... | collective-permute-start | bytes 82952 | tf_op jit(solution)/shard_map/ppermute | solution.py:18
  443.3 19.7 %copy-start.42 = (f32[32]{0:T(128)S(1)}, f32[32]{0:T(128)}, u32[]{:S(2)}) copy-start(f32[32]{0:T(128)} %param.16) | copy-start | bytes 388
  443.3 19.7 %copy-start.46 = (f32[32]{0:T(128)S(1)}, f32[32]{0:T(128)}, u32[]{:S(2)}) copy-start(f32[32]{0:T(128)} %copy-done.45) | copy-start | bytes 388
  489.5 115.4 %all-gather.15.cloned.1.call-start = ((), (), s32[]{:S(2)}) async-start(), calls=%async_computation.8 | async-start | bytes 2027520 | tf_op jit(solution)/shard_map/all_gather | solution.py:473
  500.0 12.8 %copy-start.39 = (f32[2048]{0:T(1024)S(1)}, f32[2048]{0:T(1024)}, u32[]{:S(2)}) copy-start(f32[2048]{0:T(1024)} %get-tuple-element.47) | copy-start | bytes 24580
  500.0 13.6 %copy-start.25 = (bf16[256,1024]{1,0:T(8,128)(2,1)S(1)}, bf16[256,1024]{1,0:T(8,128)(2,1)}, u32[]{:S(2)}) copy-start(bf16[256,1024]{1,0:T(8,128)(2,1)} %reduce-scatter.12.cloned.1.call-done) | copy-start | bytes 1572868
  513.5 35.0 %copy-start.38 = (f32[2048]{0:T(1024)S(1)}, f32[2048]{0:T(1024)}, u32[]{:S(2)}) copy-start(f32[2048]{0:T(1024)} %param.19) | copy-start | bytes 24580
  513.5 120.2 %reduce-scatter.14.cloned.1.call-start = ((), (), s32[]{:S(2)}) async-start(), calls=%async_computation.10 | async-start | bytes 1310720 | tf_op jit(solution)/shard_map/reduce_scatter | solution.py:467
  514.7 167.1 %reduce-scatter.20.cloned.1.call-start = ((), (), s32[]{:S(2)}) async-start(), calls=%async_computation.15 | async-start | bytes 2805760
  (30 other events, 183.4 us)
Sparse Core Ops, SparseCore 0:
  10.5 42.7 all-gather.8
  113.3 49.5 all-gather.16
  165.4 36.2 all-gather.10
  203.4 36.7 all-gather.12
  271.1 45.9 all-gather.18
  320.3 50.0 reduce-scatter.15
  374.2 51.3 reduce-scatter.11
  489.6 55.8 reduce-scatter.17
  548.7 56.1 all-gather.14
  607.8 25.9 reduce-scatter.13
  636.6 45.0 reduce-scatter.19
